TPU v7x, 32 devices: a whole 2x2x4 slice. The times are simulated.
32 devices in a mesh: dp: 8 (over z, x), hst: 4 (over y, core).
Axes of the slice: x: 2, y: 2, z: 4, core: 2. Of those that a mesh axis runs over, the one named last changes fastest.
Arguments:
- tokens: bfloat16 [128, 7168], P('dp', 'hst'), may hold values from -6 to 6
- cotangent: bfloat16 [128, 7168], P('dp', 'hst'), may hold values from -6 to 6
- expert_ids: int32 [128, 2], P('dp'), may hold values from 0 to 7, all different within a row; in each aligned block of 16 rows (0 to 15, 16 to 31, ...) at most 4 rows name the same one
- gate_values: float32 [128, 2], P('dp'), may hold values from 0.2 to 1
- w_gate: bfloat16 [8, 4864, 7168], P('hst', 'dp'), may hold values from -0.0625 to 0.0625
- w_up: bfloat16 [8, 4864, 7168], P('hst', 'dp'), may hold values from -0.0625 to 0.0625
- w_down: bfloat16 [8, 4864, 7168], P('hst', 'dp'), may hold values from -0.078125 to 0.078125
Outputs:
- mixed: bfloat16 [128, 7168], P('dp', 'hst')
- grad_tokens: bfloat16 [128, 7168], P('dp', 'hst')
- grad_gate: bfloat16 [8, 4864, 7168], P('hst', 'dp')
- grad_up: bfloat16 [8, 4864, 7168], P('hst', 'dp')
- grad_down: bfloat16 [8, 4864, 7168], P('hst', 'dp')
Inputs may be any that keep to these rules, and one draw needn't show every extreme that they name: `expert_ids`: within each block of 16 rows (the rows of one index of dp), a token names two different experts, and no expert is named by more than 4 routes; since a block has 8 routes and 8 slots, every expert fills all 4 of its slots in every block.
All inputs are finite; a program needn't handle non-finite values.
Results may differ from a plain program's by a relative error of at most 0.023.
Values may be sent and summed in bfloat16 or wider, within the bound.
No kernel may reach another device: no remote copies, remote signals or barrier semaphores. Data moves between devices by JAX's collectives and lax.ppermute only.
A program may use at most 192 MiB of HBM per device.

v0:
```python
import jax
import jax.numpy as jnp
from jax import lax
from jax.sharding import PartitionSpec as P

CAP = 4


def route_tables(expert_ids, gate_values, experts, cap):
    count = expert_ids.shape[0]
    flat = expert_ids.reshape(-1)
    labels = jnp.arange(experts, dtype=jnp.int32)
    onehot = (flat[:, None] == labels[None, :]).astype(jnp.int32)
    position = jnp.cumsum(onehot, axis=0) - onehot
    slot = jnp.sum(position * onehot, axis=1)
    slots = jnp.arange(cap, dtype=jnp.int32)
    hit = (flat[:, None, None] == labels[None, :, None]) & (
        slot[:, None, None] == slots[None, None, :]
    )
    hit = hit.astype(jnp.float32).reshape(count, 2, experts, cap)
    select = jnp.transpose(jnp.sum(hit, axis=1), (1, 2, 0))
    weigh = jnp.transpose(jnp.sum(hit * gate_values[:, :, None, None], axis=1), (1, 2, 0))
    return (select, weigh)


def body(tokens, cotangent, expert_ids, gate_values, w_gate, w_up, w_down):
    highest = lax.Precision.HIGHEST
    hosts = lax.axis_size("hst")
    local = w_gate.shape[0]
    experts = local * hosts
    select, weigh = route_tables(expert_ids, gate_values, experts, CAP)
    first = lax.axis_index("hst") * local
    mine_select = lax.dynamic_slice_in_dim(select, first, local, 0)
    mine_weigh = lax.dynamic_slice_in_dim(weigh, first, local, 0)
    x_part = jnp.einsum(
        "ecT,Td->ecd", select.astype(jnp.bfloat16), tokens, preferred_element_type=jnp.float32
    ).astype(jnp.bfloat16)
    d_part = jnp.einsum(
        "ecT,Td->ecd", weigh, cotangent.astype(jnp.float32), precision=highest
    ).astype(jnp.bfloat16)
    x_rows, d_rows = (
        lax.all_to_all(x_part, "hst", split_axis=0, concat_axis=2, tiled=True),
        lax.all_to_all(d_part, "hst", split_axis=0, concat_axis=2, tiled=True),
    )
    x_all, d_all = (
        lax.all_gather(x_rows, "dp", axis=1, tiled=True),
        lax.all_gather(d_rows, "dp", axis=1, tiled=True),
    )
    gate_act = jnp.einsum("erd,efd->erf", x_all, w_gate, preferred_element_type=jnp.float32)
    up_act = jnp.einsum("erd,efd->erf", x_all, w_up, preferred_element_type=jnp.float32)
    sigma = jax.nn.sigmoid(gate_act)
    hidden = (gate_act * sigma * up_act).astype(jnp.bfloat16)
    out_terms = jnp.einsum("erf,efd->erd", hidden, w_down, preferred_element_type=jnp.float32)
    out_rows = lax.psum_scatter(
        out_terms.astype(jnp.bfloat16), "dp", scatter_dimension=1, tiled=True
    ).astype(jnp.float32)
    d_hidden = jnp.einsum("erd,efd->erf", d_all, w_down, preferred_element_type=jnp.float32)
    d_gate = (d_hidden * up_act * sigma * (1.0 + gate_act * (1.0 - sigma))).astype(jnp.bfloat16)
    d_up = (d_hidden * gate_act * sigma).astype(jnp.bfloat16)
    grad_down = jnp.einsum(
        "erf,erd->efd", hidden, d_all, preferred_element_type=jnp.float32
    ).astype(jnp.bfloat16)
    grad_gate = jnp.einsum(
        "erf,erd->efd", d_gate, x_all, preferred_element_type=jnp.float32
    ).astype(jnp.bfloat16)
    grad_up = jnp.einsum("erf,erd->efd", d_up, x_all, preferred_element_type=jnp.float32).astype(
        jnp.bfloat16
    )
    back_terms = jnp.einsum("erf,efd->erd", d_gate, w_gate, preferred_element_type=jnp.float32)
    back_terms = back_terms + jnp.einsum(
        "erf,efd->erd", d_up, w_up, preferred_element_type=jnp.float32
    )
    back_rows = lax.psum_scatter(
        back_terms.astype(jnp.bfloat16), "dp", scatter_dimension=1, tiled=True
    ).astype(jnp.float32)
    token_terms = jnp.einsum("ecT,ecd->Td", mine_weigh, out_rows, precision=highest)
    mixed = lax.psum_scatter(
        token_terms.astype(jnp.bfloat16), "hst", scatter_dimension=1, tiled=True
    )
    grad_terms = jnp.einsum("ecT,ecd->Td", mine_select, back_rows, precision=highest)
    grad_tokens = lax.psum_scatter(
        grad_terms.astype(jnp.bfloat16), "hst", scatter_dimension=1, tiled=True
    )
    return (mixed, grad_tokens, grad_gate, grad_up, grad_down)


def solution(mesh):
    return jax.shard_map(
        body,
        mesh=mesh,
        in_specs=(
            P("dp", "hst"),
            P("dp", "hst"),
            P("dp", None),
            P("dp", None),
            P("hst", "dp", None),
            P("hst", "dp", None),
            P("hst", "dp", None),
        ),
        out_specs=(
            P("dp", "hst"),
            P("dp", "hst"),
            P("hst", "dp", None),
            P("hst", "dp", None),
            P("hst", "dp", None),
        ),
        check_vma=False,
    )
```

profile of v0, /device:TPU:0, one launch (start us, length us, event | category | flops | bytes accessed | tf_op | source)
XLA Modules:
  0.0 289.8 jit_solution(16915184036526484231)
XLA Ops:
  7.2 0.0 copy-start
  7.2 0.7 iota_compare_fusion.1
  7.9 0.8 copy.41
  8.6 0.1 eq.56
  8.7 0.1 fusion.19
  8.8 0.1 reduce_window_sum.11
  8.9 0.2 select_reduce_fusion
  9.0 0.1 eq.60
  9.1 0.1 copy.42
  9.2 0.7 fusion.16
  9.9 0.0 copy-done
  10.0 0.2 convolution_convert_fusion.5
  10.1 0.7 copy.44
  10.8 4.2 %all-to-all-start = ((bf16[8,4,1792]{2,1,0:T(4,128)(2,1)}), bf16[8,4,1792]{2,1,0:T(4,128)(2,1)S(1)}, u32[]{:S(2)}, u32[]{:S(2)}) async-start(bf16[8,4,1792]{2,1,0:T(4,128)(2,1)} %copy.44), calls=%async_computation | async-start | bytes 229376 | tf_op jit(solution)/shard_map/all_to_all | solution.py:42
  15.0 1.0 convolution_convert_fusion.4
  16.1 0.7 copy.49
  16.8 2.7 all-to-all-done
  19.5 3.3 %all-to-all-start.1 = ((bf16[8,4,1792]{2,1,0:T(4,128)(2,1)}), bf16[8,4,1792]{2,1,0:T(4,128)(2,1)S(1)}, u32[]{:S(2)}, u32[]{:S(2)}) async-start(bf16[8,4,1792]{2,1,0:T(4,128)(2,1)} %copy.49), calls=%async_computation.2 | async-start | bytes 229376 | tf_op jit(solution)/shard_map/all_to_all | solution.py:43
  22.8 0.0 all-reduce.5.cloned.1.call-start
  23.0 4.3 %all-to-all-done.1 = bf16[8,4,1792]{2,1,0:T(4,128)(2,1)S(1)} async-done(((bf16[8,4,1792]{2,1,0:T(4,128)(2,1)}), bf16[8,4,1792]{2,1,0:T(4,128)(2,1)S(1)}, u32[]{:S(2)}, u32[]{:S(2)}) %all-to-all-start.1) | async-done | bytes 114720 | tf_op jit(solution)/shard_map/all_to_all | solution.py:43
  27.3 33.4 %all_gather.6 = bf16[2,32,7168]{2,0,1:T(2,128)(2,1)S(1)} all-gather(bf16[2,4,7168]{2,0,1:T(2,128)(2,1)S(1)} %all_to_all.29), channel_id=1, replica_groups=mesh['dp'=8,'hst'=4] {'dp'}, dimensions={1}, use_global_device_ids=true | all-gather | bytes 1032192 | tf_op jit(solution)/shard_map/all_gather | solution.py:46
  60.8 8.6 %fusion.8 = f32[2,32,608]{2,1,0:T(8,128)S(1)} fusion(bf16[2,608,7168]{2,1,0:T(8,128)(2,1)} %param.12, bf16[2,32,7168]{2,0,1:T(2,128)(2,1)S(1)} %all_gather.6), kind=kOutput, calls=%fused_computation.17 | convolution fusion | flops 557842432 | bytes 18505728 | tf_op jit(solution)/shard_map/erd,efd->erf/dot_general | solution.py:50
  69.4 8.7 %fusion.10 = f32[2,32,608]{2,1,0:T(8,128)S(1)} fusion(bf16[2,608,7168]{2,1,0:T(8,128)(2,1)} %param.11, bf16[2,32,7168]{2,0,1:T(2,128)(2,1)S(1)} %all_gather.6), kind=kOutput, calls=%fused_computation.19 | convolution fusion | flops 557842432 | bytes 18505728 | tf_op jit(solution)/shard_map/erd,efd->erf/dot_general | solution.py:49
  78.1 32.2 %all_gather.7 = bf16[2,32,7168]{2,0,1:T(2,128)(2,1)S(1)} all-gather(bf16[2,4,7168]{2,0,1:T(2,128)(2,1)S(1)} %all_to_all.33), channel_id=1, replica_groups=mesh['dp'=8,'hst'=4] {'dp'}, dimensions={1}, use_global_device_ids=true | all-gather | bytes 1032192 | tf_op jit(solution)/shard_map/all_gather | solution.py:47
  110.3 8.6 %multiply_convert_fusion = (bf16[2,32,608]{2,1,0:T(8,128)(2,1)S(1)}, bf16[2,32,608]{2,1,0:T(8,128)(2,1)S(1)}, bf16[2,32,608]{2,1,0:T(8,128)(2,1)S(1)}) fusion(f32[2,32,608]{2,1,0:T(8,128)S(1)} %fusion.10, f32[2,32,608]{2,1,0:T(8,128)S(1)} %fusion.8, bf16[2,608,7168]{2,1,0:T(8,128)(2,1)} %param.13, bf16[2,32,7168]{2,0,1:T(2,128)(2,1)S(1)} %all_gather.7), kind=kOutput, calls=%fused_computation.21 | convolution fusion | flops 558465024 | bytes 18894848 | tf_op jit(solution)/shard_map/erd,efd->erf/dot_general | solution.py:57
  118.9 0.0 slice-start
  118.9 0.0 slice-start.1
  118.9 0.0 slice-start.2
  118.9 10.1 %convolution_convert_fusion.3 = bf16[2,32,7168]{2,1,0:T(8,128)(2,1)} fusion(bf16[2,32,608]{2,1,0:T(8,128)(2,1)S(1)} %get-tuple-element.11, bf16[2,608,7168]{2,1,0:T(8,128)(2,1)} %param.13), kind=kOutput, calls=%fused_computation.5 | convolution fusion | flops 558301184 | bytes 18427904 | tf_op jit(solution)/shard_map/erf,efd->erd/dot_general | solution.py:53
  129.1 0.0 slice-start.3
  129.1 0.0 slice-start.4
  129.1 7.7 %fusion.24 = f32[2,32,7168]{2,1,0:T(8,128)S(1)} fusion(bf16[2,32,608]{2,1,0:T(8,128)(2,1)S(1)} %get-tuple-element.10, bf16[2,608,7168]{2,1,0:T(8,128)(2,1)} %param.11), kind=kOutput, calls=%fused_computation.47 | convolution fusion | flops 557842432 | bytes 19345408 | tf_op jit(solution)/shard_map/erf,efd->erd/dot_general | solution.py:69
  136.7 0.0 copy-start.2
  136.8 0.0 slice-done
  136.8 0.0 slice-done.1
  136.8 0.0 slice-done.2
  136.8 0.0 slice-done.3
  136.8 0.0 slice-done.4
  136.8 4.0 %fusion = bf16[2,32,7168]{2,1,0:T(8,128)(2,1)} fusion(f32[2,32,7168]{2,1,0:T(8,128)S(1)} %fusion.24, bf16[2,32,608]{2,1,0:T(8,128)(2,1)S(1)} %get-tuple-element.9, bf16[2,608,7168]{2,1,0:T(8,128)(2,1)S(1)} %bitcast.54), kind=kOutput, calls=%fused_computation.4 | convolution fusion | flops 558759936 | bytes 20262912 | tf_op jit(solution)/shard_map/erf,efd->erd/dot_general | solution.py:70
  140.8 0.0 all-reduce.5.cloned.1.call-update
  140.8 0.0 reduce-scatter.7.cloned.1.call-start
  140.9 0.0 copy-done.2
  140.9 0.6 dynamic-slice.8
  142.2 8.9 %convolution_convert_fusion = bf16[2,608,7168]{2,1,0:T(8,128)(2,1)} fusion(bf16[2,32,608]{2,1,0:T(8,128)(2,1)S(1)} %get-tuple-element.11, bf16[2,32,7168]{2,0,1:T(2,128)(2,1)S(1)} %all_gather.7), kind=kOutput, calls=%fused_computation | convolution fusion | flops 566558720 | bytes 18427904 | tf_op jit(solution)/shard_map/erf,erd->efd/dot_general | solution.py:60
  151.0 86.7 %all-reduce.5.cloned.1.call-done = (bf16[2,32,7168]{2,1,0:T(8,128)(2,1)}, bf16[2,32,7168]{2,1,0:T(8,128)(2,1)}) async-done(((bf16[2,32,7168]{2,1,0:T(8,128)(2,1)}, bf16[2,32,7168]{2,1,0:T(8,128)(2,1)}), (bf16[2,32,7168]{2,1,0:T(8,128)(2,1)}, bf16[2,32,7168]{2,1,0:T(8,128)(2,1)})) %all-reduce.5.cloned.1.call-update) | async-done | bytes 1835024
  237.7 2.1 fusion.2
  239.8 0.0 reduce-scatter.7.cloned.1.call-update
  239.8 0.0 copy-start.1
  239.8 0.3 reduce-scatter.5.cloned.1.call-start
  240.1 8.9 %convolution_convert_fusion.1 = bf16[2,608,7168]{2,1,0:T(8,128)(2,1)} fusion(bf16[2,32,608]{2,1,0:T(8,128)(2,1)S(1)} %get-tuple-element.9, bf16[2,32,7168]{2,0,1:T(2,128)(2,1)S(1)} %all_gather.6), kind=kOutput, calls=%fused_computation.1 | convolution fusion | flops 566558720 | bytes 18427904 | tf_op jit(solution)/shard_map/erf,erd->efd/dot_general | solution.py:66
  249.0 2.1 fusion.1
  251.0 0.0 reduce-scatter.5.cloned.1.call-update
  251.1 8.9 %convolution_convert_fusion.2 = bf16[2,608,7168]{2,1,0:T(8,128)(2,1)} fusion(bf16[2,32,608]{2,1,0:T(8,128)(2,1)S(1)} %get-tuple-element.10, bf16[2,32,7168]{2,0,1:T(2,128)(2,1)S(1)} %all_gather.6), kind=kOutput, calls=%fused_computation.2 | convolution fusion | flops 566558720 | bytes 18427904 | tf_op jit(solution)/shard_map/erf,erd->efd/dot_general | solution.py:63
  259.9 0.4 reduce-scatter.7.cloned.1.call-done
  260.3 22.9 %reduce-scatter.5.cloned.1.call-done = bf16[16,1792]{1,0:T(8,128)(2,1)} async-done(((bf16[16,7168]{1,0:T(8,128)(2,1)}), bf16[16,1792]{1,0:T(8,128)(2,1)}) %reduce-scatter.5.cloned.1.call-update) | async-done | bytes 57360 | tf_op jit(solution)/shard_map/reduce_scatter | solution.py:77
  283.2 0.0 copy-done.1
  (8 shorter events, 0.2 us)
Async XLA Ops:
  7.2 2.8 copy-start
  10.8 8.7 %all-to-all-start = ((bf16[8,4,1792]{2,1,0:T(4,128)(2,1)}), bf16[8,4,1792]{2,1,0:T(4,128)(2,1)S(1)}, u32[]{:S(2)}, u32[]{:S(2)}) async-start(bf16[8,4,1792]{2,1,0:T(4,128)(2,1)} %copy.44), calls=%async_computation | async-start | bytes 229376 | tf_op jit(solution)/shard_map/all_to_all | solution.py:42
  19.5 7.7 %all-to-all-start.1 = ((bf16[8,4,1792]{2,1,0:T(4,128)(2,1)}), bf16[8,4,1792]{2,1,0:T(4,128)(2,1)S(1)}, u32[]{:S(2)}, u32[]{:S(2)}) async-start(bf16[8,4,1792]{2,1,0:T(4,128)(2,1)} %copy.49), calls=%async_computation.2 | async-start | bytes 229376 | tf_op jit(solution)/shard_map/all_to_all | solution.py:43
  22.8 214.9 %all-reduce.5.cloned.1.call-start = ((), (), s32[]{:S(2)}) async-start(), calls=%async_computation.6 | async-start | bytes 3670016
  118.9 17.8 %slice-start = ((s8[17432576]{0:T(1024)(128)(4,1)}), s8[4194304]{0:T(1024)(128)(4,1)S(1)}, s32[]{:S(2)}) async-start(s8[17432576]{0:T(1024)(128)(4,1)} %bitcast.53), calls=%async_computation.7 | async-start | bytes 8388608
  118.9 17.8 %slice-start.1 = ((s8[17432576]{0:T(1024)(128)(4,1)}), s8[4194304]{0:T(1024)(128)(4,1)S(1)}, s32[]{:S(2)}) async-start(s8[17432576]{0:T(1024)(128)(4,1)} %bitcast.53), calls=%async_computation.8 | async-start | bytes 8388608
  118.9 17.8 %slice-start.2 = ((s8[17432576]{0:T(1024)(128)(4,1)}), s8[4194304]{0:T(1024)(128)(4,1)S(1)}, s32[]{:S(2)}) async-start(s8[17432576]{0:T(1024)(128)(4,1)} %bitcast.53), calls=%async_computation.9 | async-start | bytes 8388608
  129.1 7.7 %slice-start.3 = ((s8[17432576]{0:T(1024)(128)(4,1)}), s8[4194304]{0:T(1024)(128)(4,1)S(1)}, s32[]{:S(2)}) async-start(s8[17432576]{0:T(1024)(128)(4,1)} %bitcast.53), calls=%async_computation.10 | async-start | bytes 8388608
  129.1 7.7 %slice-start.4 = ((s8[17432576]{0:T(1024)(128)(4,1)}), s8[655360]{0:T(1024)(128)(4,1)S(1)}, s32[]{:S(2)}) async-start(s8[17432576]{0:T(1024)(128)(4,1)} %bitcast.53), calls=%async_computation.11 | async-start | bytes 1310720
  136.7 4.2 %copy-start.2 = (u32[32]{0:T(128)S(1)}, u32[32]{0:T(128)}, u32[]{:S(2)}) copy-start(u32[32]{0:T(128)} %constant.24) | copy-start | bytes 388
  140.8 119.5 %reduce-scatter.7.cloned.1.call-start = ((), (), s32[]{:S(2)}) async-start(), calls=%async_computation.5 | async-start | bytes 286720 | tf_op jit(solution)/shard_map/reduce_scatter | solution.py:81
  239.8 43.4 %copy-start.1 = (bf16[16,1792]{1,0:T(8,128)(2,1)S(1)}, bf16[16,1792]{1,0:T(8,128)(2,1)}, u32[]{:S(2)}) copy-start(bf16[16,1792]{1,0:T(8,128)(2,1)} %param.7) | copy-start | bytes 172036
  239.8 43.4 %reduce-scatter.5.cloned.1.call-start = ((), (), s32[]{:S(2)}) async-start(), calls=%async_computation.4 | async-start | bytes 286720 | tf_op jit(solution)/shard_map/reduce_scatter | solution.py:77
Sparse Core Ops, SparseCore 0:
  141.0 96.7 all-reduce.4
  240.7 19.5 reduce-scatter.6
  263.3 19.8 reduce-scatter.4
where the time goes:
time: 290 us
  waiting for transfers between devices  117 us (40%)
  matrix products  79.7 us (27%)
  blocking collectives  65.6 us (23%)
  between operations  14.6 us (5%)
  starting transfers between devices  7.9 us (3%)
  local copies, waits for them, and re-layouts  3.24 us (1%)
    unnamed x4, waiting for transfers between devices  86.7 us
    all_gather x1, blocking collectives, body(): lax.all_gather(x_rows, 'dp', axis=1, tiled=True)  33.4 us
    all_gather x1, blocking collectives, body(): lax.all_gather(d_rows, 'dp', axis=1, tiled=True)  32.2 us
    reduce_scatter x1, waiting for transfers between devices, body(): lax.psum_scatter(token_terms.astype(jnp.bfloat16), 'hst', scatter_dimensi...  22.9 us
    dot_general x1, matrix products, body(): jnp.einsum('erf,efd->erd', hidden, w_down, preferred_element_type=jnp.flo...  10.1 us
    dot_general x1, matrix products, body(): jnp.einsum('erf,erd->efd', hidden, d_all, preferred_element_type=jnp.floa...  8.86 us
    dot_general x1, matrix products, body(): jnp.einsum('erf,erd->efd', d_gate, x_all, preferred_element_type=jnp.floa...  8.86 us
    dot_general x1, matrix products, body(): jnp.einsum('erf,erd->efd', d_up, x_all, preferred_element_type=jnp.float32)  8.85 us
  transfers between devices with their start and end apart: 5, of which 5 were waited for; matrix products, arithmetic and copies ran while one was open for 11% of the time, Pallas kernels for 0%

commit v1 on v0

v1 whole, which is shorter than its diff:
```python
import functools

import jax
import jax.numpy as jnp
from jax import lax
from jax.experimental import pallas as pl
from jax.experimental.pallas import tpu as pltpu
from jax.sharding import PartitionSpec as P

CAP = 4
LANES = 128
MIB = 1 << 20
F32 = jnp.float32
BF16 = jnp.bfloat16
AXES = ("dp", "hst")


def dot(a, b):
    return lax.dot_general(a, b, (((1,), (0,)), ((), ())), preferred_element_type=F32)


def dot_t(a, b):
    return lax.dot_general(a, b, (((1,), (1,)), ((), ())), preferred_element_type=F32)


def log2(n):
    assert n & (n - 1) == 0
    return n.bit_length() - 1


class Grid:
    def __init__(self, dp, hst):
        self.dp, self.hst = dp, hst
        self.nc = 2 if hst % 2 == 0 else 1
        self.ny = hst // self.nc
        self.nx = self.ny if dp % self.ny == 0 else 1
        self.nz = dp // self.nx
        self.square = [(a, b) for a in range(self.nx) for b in range(self.ny)]

    def shift(self, value, dz=0, dx=0, dy=0, dc=0):
        pairs = []
        for z in range(self.nz):
            for x in range(self.nx):
                for y in range(self.ny):
                    for c in range(self.nc):
                        to_dp = (z + dz) % self.nz * self.nx + (x + dx) % self.nx
                        to_hst = (y + dy) % self.ny * self.nc + (c + dc) % self.nc
                        here = (z * self.nx + x) * self.hst + y * self.nc + c
                        pairs.append((here, to_dp * self.hst + to_hst))
        return lax.ppermute(value, AXES, pairs)


def gather(grid, mine):
    parts = [mine] + [grid.shift(mine, dz=k) for k in range(1, grid.nz)]
    column = jnp.concatenate(parts, axis=0)
    plane = {
        (a, b): column if (a, b) == (0, 0) else grid.shift(column, dx=a, dy=b)
        for a, b in grid.square
    }
    planes = [plane]
    for c in range(1, grid.nc):
        planes.append({at: grid.shift(block, dc=c) for at, block in plane.items()})
    return planes


def scatter_sum(grid, parts, rows):
    kept = parts[0].astype(F32)
    for c in range(1, grid.nc):
        kept = kept + grid.shift(parts[c], dc=-c).astype(F32)
    kept = kept.astype(BF16)
    total = kept[0, 0].astype(F32)
    for a, b in grid.square[1:]:
        total = total + grid.shift(kept[a, b], dx=-a, dy=-b).astype(F32)
    total = total.astype(BF16)
    result = total[:rows].astype(F32)
    for k in range(1, grid.nz):
        block = lax.slice_in_dim(total, k * rows, (k + 1) * rows, axis=0)
        result = result + grid.shift(block, dz=-k).astype(F32)
    return result.astype(BF16)


def tables(aux, first, rows, local, block):
    tokens = aux.shape[0]
    across = jnp.transpose(aux.astype(F32))
    ids = [across[k : k + 1] for k in range(2)]
    gates = [across[2 + k : 3 + k] + across[4 + k : 5 + k] + across[6 + k : 7 + k] for k in range(2)]
    total = local * rows
    r = lax.broadcasted_iota(jnp.int32, (total, tokens), 0)
    j = lax.broadcasted_iota(jnp.int32, (total, tokens), 1)
    expert = ((r >> log2(rows)) + first).astype(F32)
    own_block = ((r & (rows - 1)) >> log2(CAP)) == (j >> log2(block))
    slot = (r & (CAP - 1)).astype(F32)
    hits = [(ids[k] == expert).astype(F32) for k in range(2)]
    hit = hits[0] + hits[1]
    up = lax.broadcasted_iota(jnp.int32, (tokens, tokens), 0)
    to = lax.broadcasted_iota(jnp.int32, (tokens, tokens), 1)
    earlier = ((up >> log2(block)) == (to >> log2(block))) & (up < to)
    position = dot(hit.astype(BF16), jnp.where(earlier, 1.0, 0.0).astype(BF16))
    select = jnp.where(own_block & (position == slot), hit, 0.0)
    gate = jnp.sum(select * (hits[0] * gates[0] + hits[1] * gates[1]), axis=1, keepdims=True)
    return select, gate


def route(blocks, select, out_ref, width, chunk):
    index = 0
    for plane in blocks:
        for group in plane:
            whole = jnp.concatenate([ref[:, :width] for ref in group], axis=0)
            picked = dot(select, whole)
            for at in range(0, width, chunk):
                yield index, picked[:, at : at + chunk]
                index += 1


def first_kernel(shape, place_ref, *refs):
    grid, local, rows, block, width, chunk, chunks = shape
    count = grid.nc * grid.ny * grid.nx
    it = iter(refs[:count])
    blocks = [[[next(it) for _ in range(grid.nx)] for _ in range(grid.ny)] for _ in range(grid.nc)]
    (wg_ref, wu_ref, x_ref, select_ref, back_ref, gate_ref, act_ref, p_ref, q_ref, g_acc, u_acc) = refs[count:]
    step = pl.program_id(0)

    @pl.when(step == 0)
    def _():
        aux = jnp.concatenate([ref[:, width : width + LANES] for ref in blocks[0][0]], axis=0)
        select, gate = tables(aux, place_ref[chunks], rows, local, block)
        gate_ref[...] = jnp.broadcast_to(gate, gate_ref.shape)
        select_ref[...] = select.astype(BF16)
        back_ref[...] = jnp.transpose(select).astype(BF16)
        for index, picked in route(blocks, select.astype(BF16), x_ref, width, chunk):
            x_ref[index] = picked.astype(BF16)
        g_acc[...] = jnp.zeros_like(g_acc)
        u_acc[...] = jnp.zeros_like(u_acc)

    x = x_ref[step]
    for e in range(local):
        mine = x[e * rows : (e + 1) * rows]
        g_acc[e] += dot_t(mine, wg_ref[e])
        u_acc[e] += dot_t(mine, wu_ref[e])

    @pl.when(step == chunks - 1)
    def _():
        g, u = g_acc[...], u_acc[...]
        sigma = jax.nn.sigmoid(g)
        act_ref[...] = (g * sigma * u).astype(BF16)
        p_ref[...] = u * sigma * (1.0 + g * (1.0 - sigma))
        q_ref[...] = g * sigma


def forward_kernel(local, rows, half, place_ref, act_ref, gate_ref, back_ref, w_ref, own_ref, other_ref, o_rows):
    step = pl.program_id(0)
    for e in range(local):
        at = slice(e * rows, (e + 1) * rows)
        o_rows[at] = (dot(act_ref[e], w_ref[e]) * gate_ref[at, :1]).astype(BF16)
    put(step, half, dot(back_ref[...], o_rows[...]).astype(BF16), own_ref, other_ref)


def put(step, half, value, own_ref, other_ref):
    @pl.when(step < half)
    def _():
        own_ref[...] = value.reshape(own_ref.shape)

    @pl.when(step >= half)
    def _():
        other_ref[...] = value.reshape(other_ref.shape)


def second_kernel(shape, place_ref, *refs):
    grid, local, rows, block, width, chunk, chunks = shape
    count = grid.nc * grid.ny * grid.nx
    it = iter(refs[:count])
    blocks = [[[next(it) for _ in range(grid.nx)] for _ in range(grid.ny)] for _ in range(grid.nc)]
    (select_ref, gate_ref, p_ref, q_ref, w_ref, d_ref, dg_ref, du_ref, acc) = refs[count:]
    step = pl.program_id(0)

    @pl.when(step == 0)
    def _():
        for index, picked in route(blocks, select_ref[...], d_ref, width, chunk):
            d_ref[index] = (picked * gate_ref[:, :1]).astype(BF16)
        acc[...] = jnp.zeros_like(acc)

    d = d_ref[step]
    for e in range(local):
        acc[e] += dot_t(d[e * rows : (e + 1) * rows], w_ref[e])

    @pl.when(step == chunks - 1)
    def _():
        da = acc[...]
        dg_ref[...] = (da * p_ref[...]).astype(BF16)
        du_ref[...] = (da * q_ref[...]).astype(BF16)


def back_kernel(local, rows, half, place_ref, dg_ref, du_ref, back_ref, wg_ref, wu_ref, own_ref, other_ref, o_rows):
    step = pl.program_id(0)
    for e in range(local):
        at = slice(e * rows, (e + 1) * rows)
        o_rows[at] = (dot(dg_ref[e], wg_ref[e]) + dot(du_ref[e], wu_ref[e])).astype(BF16)
    put(step, half, dot(back_ref[...], o_rows[...]).astype(BF16), own_ref, other_ref)


def grads_kernel(local, rows, count, place_ref, *refs):
    lefts, (rows_ref,) = refs[:count], refs[count : count + 1]
    outs, turned = refs[count + 1 : 2 * count + 1], refs[2 * count + 1 :]

    @pl.when(pl.program_id(0) == 0)
    def _():
        for left, turn in zip(lefts, turned):
            for e in range(local):
                turn[e] = jnp.transpose(left[e].astype(F32)).astype(BF16)

    right = rows_ref[0]
    for turn, out in zip(turned, outs):
        for e in range(local):
            out[e] = dot(turn[e], right[e * rows : (e + 1) * rows]).astype(BF16)


def body(tokens, cotangent, expert_ids, gate_values, w_gate, w_up, w_down):
    grid = Grid(lax.axis_size("dp"), lax.axis_size("hst"))
    local, hidden, features = w_gate.shape
    block, width = tokens.shape
    rows = grid.dp * CAP
    total = local * rows
    chunk = 896 if width % 896 == 0 else width
    per = width // chunk
    chunks = features // chunk
    half = chunks // grid.nc
    count = grid.dp * block
    column = grid.nz * block
    shape = (grid, local, rows, block, width, chunk, chunks)

    host = lax.axis_index("hst")
    y, core = host // grid.nc, host % grid.nc
    i = jnp.arange(chunks, dtype=jnp.int32)
    dc, dy, sub = i // (per * grid.ny), i // per % grid.ny, i % per
    source = ((y - dy) % grid.ny) * grid.nc + (core + dc) % grid.nc
    place = jnp.concatenate([source * per + sub, (host * local)[None]]).astype(jnp.int32)

    high = lax.reduce_precision(gate_values, 8, 7)
    rest = gate_values - high
    middle = lax.reduce_precision(rest, 8, 7)
    aux = jnp.concatenate([expert_ids.astype(F32), high, middle, rest - middle], axis=1)
    aux = jnp.pad(aux.astype(BF16), ((0, 0), (0, LANES - aux.shape[1])))
    x_planes = gather(grid, jnp.concatenate([tokens, aux], axis=1))
    d_planes = gather(grid, cotangent)

    def flat(planes):
        return [p[a, b] for p in planes for b in range(grid.ny) for a in range(grid.nx)]

    whole = lambda *dims: pl.BlockSpec(dims, lambda i, place: (0,) * len(dims))
    weight = pl.BlockSpec((local, hidden, chunk), lambda i, place: (0, 0, place[i]))
    hidden_shape = (local, rows, hidden)
    sums = (grid.nx, grid.ny, column, width)
    sum_block = (grid.nx, 1, column, chunk)
    own = pl.BlockSpec(sum_block, lambda i, place: (0, jnp.minimum(i, half - 1) // per, 0, jnp.minimum(i, half - 1) % per))
    other = pl.BlockSpec(sum_block, lambda i, place: (0, jnp.maximum(i - half, 0) // per, 0, jnp.maximum(i - half, 0) % per))
    pass_flops = 2 * total * hidden * features
    pass_bytes = 2 * local * hidden * features

    def call(kernel, name, ins, outs, args, scratch=(), passes=1, limit=40):
        return pl.pallas_call(
            kernel,
            name=name,
            out_shape=[o[0] for o in outs],
            grid_spec=pltpu.PrefetchScalarGridSpec(
                num_scalar_prefetch=1,
                grid=(chunks,),
                in_specs=ins,
                out_specs=[o[1] for o in outs],
                scratch_shapes=list(scratch),
            ),
            compiler_params=pltpu.CompilerParams(
                dimension_semantics=("arbitrary",), vmem_limit_bytes=limit * MIB
            ),
            cost_estimate=pl.CostEstimate(
                flops=passes * pass_flops, bytes_accessed=passes * pass_bytes, transcendentals=0
            ),
        )(place, *args)

    def full(dtype, *dims):
        return (jax.ShapeDtypeStruct(dims, dtype), whole(*dims))

    x_blocks, d_blocks = flat(x_planes), flat(d_planes)
    routed = full(BF16, chunks, total, chunk)
    x_rows, select, back, gate, act, p, q = call(
        functools.partial(first_kernel, shape),
        "gate_up",
        [whole(column, width + LANES)] * len(x_blocks) + [weight, weight],
        [
            routed,
            full(BF16, total, count),
            full(BF16, count, total),
            full(F32, total, LANES),
            full(BF16, *hidden_shape),
            full(F32, *hidden_shape),
            full(F32, *hidden_shape),
        ],
        [*x_blocks, w_gate, w_up],
        [pltpu.VMEM(hidden_shape, F32)] * 2,
        passes=2,
    )
    partial_sums = [(jax.ShapeDtypeStruct(sums, BF16), own), (jax.ShapeDtypeStruct(sums, BF16), other)]
    picked = [pltpu.VMEM((total, chunk), BF16)]
    out_parts = call(
        functools.partial(forward_kernel, local, rows, half),
        "forward",
        [whole(*hidden_shape), whole(total, LANES), whole(count, total), weight],
        partial_sums,
        [act, gate, back, w_down],
        picked,
    )
    mixed = scatter_sum(grid, out_parts, block)
    d_rows, d_gate, d_up = call(
        functools.partial(second_kernel, shape),
        "hidden_grads",
        [whole(column, width)] * len(d_blocks)
        + [whole(total, count), whole(total, LANES), whole(*hidden_shape), whole(*hidden_shape), weight],
        [routed, full(BF16, *hidden_shape), full(BF16, *hidden_shape)],
        [*d_blocks, select, gate, p, q, w_down],
        [pltpu.VMEM(hidden_shape, F32)],
    )
    back_parts = call(
        functools.partial(back_kernel, local, rows, half),
        "backward",
        [whole(*hidden_shape), whole(*hidden_shape), whole(count, total), weight, weight],
        partial_sums,
        [d_gate, d_up, back, w_gate, w_up],
        picked,
        passes=2,
    )
    grad_tokens = scatter_sum(grid, back_parts, block)

    def grads(name, lefts, right):
        return call(
            functools.partial(grads_kernel, local, rows, len(lefts)),
            name,
            [whole(*hidden_shape)] * len(lefts) + [pl.BlockSpec((1, total, chunk), lambda i, place: (i, 0, 0))],
            [(jax.ShapeDtypeStruct(w_gate.shape, BF16), weight)] * len(lefts),
            [*lefts, right],
            [pltpu.VMEM((local, hidden, rows), BF16)] * len(lefts),
            passes=len(lefts),
        )

    (grad_down,) = grads("grad_down", [act], d_rows)
    grad_gate, grad_up = grads("grad_gate_up", [d_gate, d_up], x_rows)
    return mixed, grad_tokens, grad_gate, grad_up, grad_down


def solution(mesh):
    return jax.shard_map(
        body,
        mesh=mesh,
        in_specs=(
            P("dp", "hst"),
            P("dp", "hst"),
            P("dp", None),
            P("dp", None),
            P("hst", "dp", None),
            P("hst", "dp", None),
            P("hst", "dp", None),
        ),
        out_specs=(
            P("dp", "hst"),
            P("dp", "hst"),
            P("hst", "dp", None),
            P("hst", "dp", None),
            P("hst", "dp", None),
        ),
        check_vma=False,
    )
```

time: 290 us -> 162 us (0.56)
  matrix products: 79.7 us -> 0 us
  Pallas kernels: 0 us -> 79.5 us
  waiting for transfers between devices: 117 us -> 44.5 us
  blocking collectives: 65.6 us -> 0 us
  starting transfers between devices: 7.9 us -> 29.9 us
  between operations: 14.6 us -> 0.81 us
  other arithmetic: 1.73 us -> 5.19 us
    unnamed x4 -> x0, waiting for transfers between devices: 86.7 us -> none
    dot_general x13 -> x0, matrix products: 79.7 us -> none  [the longest x1 10.1 us: body(): jnp.einsum('erf,efd->erd', hidden, w_down, preferred_element_type=jnp.flo...]
    pallas_call x0 -> x6, Pallas kernels: none -> 79.5 us  [call(): pl.pallas_call(kernel, name=name, out_shape=[o[0] for o in outs], grid_sp...]
    all_gather x2 -> x0, blocking collectives: 65.6 us -> none  [the longest x1 33.4 us: body(): lax.all_gather(x_rows, 'dp', axis=1, tiled=True)]
    ppermute x0 -> x34, waiting for transfers between devices: none -> 44.5 us  [shift(): return lax.ppermute(value, AXES, pairs)]
    ppermute x0 -> x34, starting transfers between devices: none -> 29.9 us  [shift(): return lax.ppermute(value, AXES, pairs)]
    reduce_scatter x2 -> x0, waiting for transfers between devices: 23.3 us -> none  [the longest x1 22.9 us: body(): lax.psum_scatter(token_terms.astype(jnp.bfloat16), 'hst', scatter_dimensi...]
    all_to_all x2 -> x0, starting transfers between devices: 7.55 us -> none  [the longest x1 4.24 us: body(): lax.all_to_all(x_part, 'hst', split_axis=0, concat_axis=2, tiled=True)]
  transfers between devices with their start and end apart: 5 -> 34, of which waited for: 5 -> 17; matrix products, arithmetic and copies ran while one was open for 11% -> 2% of each run, Pallas kernels for 0% -> 49%
where the time goes in v1:
time: 162 us
  Pallas kernels  79.5 us (49%)
  waiting for transfers between devices  44.5 us (27%)
  starting transfers between devices  29.9 us (18%)
  other arithmetic  5.19 us (3%)
  local copies, waits for them, and re-layouts  1.9 us (1%)
    pallas_call x6, Pallas kernels, call(): pl.pallas_call(kernel, name=name, out_shape=[o[0] for o in outs], grid_sp...  79.5 us
    ppermute x34, waiting for transfers between devices, shift(): return lax.ppermute(value, AXES, pairs)  44.5 us
    ppermute x34, starting transfers between devices, shift(): return lax.ppermute(value, AXES, pairs)  29.9 us
  transfers between devices with their start and end apart: 34, of which 17 were waited for; matrix products, arithmetic and copies ran while one was open for 2% of the time, Pallas kernels for 49%

profile of v1, /device:TPU:0, one launch (start us, length us, event | category | flops | bytes accessed | tf_op | source)
XLA Modules:
  0.0 161.8 jit_solution(13668456632232166774)
XLA Ops:
  0.6 0.8 copy.16
  1.4 0.7 reduce_precision.6
  2.1 0.1 copy.15
  2.2 0.7 convert_convert_fusion
  2.8 0.1 copy.18
  2.9 0.1 fusion.13
  3.0 0.8 pad_maximum_fusion.1
  3.9 5.0 %collective-permute-start.2 = (bf16[16,1920]{1,0:T(8,128)(2,1)S(1)}, bf16[16,1920]{1,0:T(8,128)(2,1)S(1)}, u32[]{:S(2)}, u32[]{:S(2)}) collective-permute-start(bf16[16,1920]{1,0:T(8,128)(2,1)S(1)} %pad_maximum_fusion.1), channel_id=1, source_target_pairs={{0,24},{1,25},{2,26},{3,27},{4,28},{5,29},{6,30},{7,31},{8,0},{9,1... | collective-permute-start | bytes 184328 | tf_op jit(solution)/shard_map/ppermute | solution.py:50
  8.9 1.0 collective-permute-start
  9.9 2.5 %collective-permute-start.17 = (bf16[16,1792]{1,0:T(8,128)(2,1)}, bf16[16,1792]{1,0:T(8,128)(2,1)S(1)}, u32[]{:S(2)}, u32[]{:S(2)}) collective-permute-start(bf16[16,1792]{1,0:T(8,128)(2,1)} %param.8), channel_id=1, source_target_pairs={{0,8},{1,9},{2,10},{3,11},{4,12},{5,13},{6,14},{7,15},{8,16},{9,17... | collective-permute-start | bytes 172040 | tf_op jit(solution)/shard_map/ppermute | solution.py:50
  12.4 0.9 collective-permute-start.18
  13.3 4.7 %collective-permute-done.1 = bf16[16,1920]{1,0:T(8,128)(2,1)S(1)} collective-permute-done((bf16[16,1920]{1,0:T(8,128)(2,1)S(1)}, bf16[16,1920]{1,0:T(8,128)(2,1)S(1)}, u32[]{:S(2)}, u32[]{:S(2)}) %collective-permute-start.1) | collective-permute-done | bytes 61472 | tf_op jit(solution)/shard_map/ppermute | solution.py:50
  18.0 0.8 pad_maximum_fusion.refs_0_
  18.8 1.6 collective-permute-start.3
  20.4 1.5 collective-permute-start.4
  21.9 0.5 collective-permute-start.5
  22.4 0.8 constant_dynamic-update-slice_fusion.3
  23.2 0.1 pad_add_fusion.place_ref
  23.3 0.0 collective-permute-start.6
  23.3 4.5 %collective-permute-done.3.refs_1_ = bf16[64,1920]{1,0:T(8,128)(2,1)S(1)} collective-permute-done((bf16[64,1920]{1,0:T(8,128)(2,1)S(1)}, bf16[64,1920]{1,0:T(8,128)(2,1)S(1)}, u32[]{:S(2)}, u32[]{:S(2)}) %collective-permute-start.3) | collective-permute-done | bytes 245792 | tf_op jit(solution)/shard_map/ppermute | solution.py:50
  27.8 3.9 %collective-permute-done.4.refs_2_ = bf16[64,1920]{1,0:T(8,128)(2,1)S(1)} collective-permute-done((bf16[64,1920]{1,0:T(8,128)(2,1)S(1)}, bf16[64,1920]{1,0:T(8,128)(2,1)S(1)}, u32[]{:S(2)}, u32[]{:S(2)}) %collective-permute-start.4) | collective-permute-done | bytes 245792 | tf_op jit(solution)/shard_map/ppermute | solution.py:50
  31.7 0.5 collective-permute-start.9
  32.2 0.1 collective-permute-start.19
  32.3 0.9 collective-permute-done.8.refs_6_
  33.2 0.4 collective-permute-done.9.refs_7_
  33.6 17.6 %gate_up.1 = (bf16[8,64,896]{2,1,0:T(8,128)(2,1)S(1)}, bf16[64,128]{1,0:T(8,128)(2,1)S(1)}, bf16[128,64]{1,0:T(8,128)(2,1)S(1)}, f32[64,128]{1,0:T(8,128)S(1)}, ...) custom-call(s32[9]{0:T(128)S(1)} %pad_add_fusion.place_ref, ...), custom_call_target="tpu_custom_call" | custom-call | flops 1115684864 | bytes 34865152 | tf_op jit(solution)/shard_map/gate_up/pallas_call | solution.py:260
  51.2 11.0 %forward.1 = (bf16[2,2,64,1792]{3,2,1,0:T(8,128)(2,1)S(1)}, bf16[2,2,64,1792]{3,2,1,0:T(8,128)(2,1)S(1)}) custom-call(s32[9]{0:T(128)S(1)} %pad_add_fusion.place_ref, bf16[2,32,608]{2,1,0:T(8,128)(2,1)S(1)} %get-tuple-element.21.act_ref.refs_0_, f32[64,128]{1,0:T(8,128)S(1)} %get-tuple-element.22.gate_ref.refs_9_, ...), custom_call_target="tpu_custom_call" | custom-call | flops 557842432 | bytes 17432576 | tf_op jit(solution)/shard_map/forward/pallas_call | solution.py:260
  62.2 0.2 collective-permute-start.10
  62.5 0.9 collective-permute-start.20
  63.4 1.2 collective-permute-start.21
  64.6 1.4 collective-permute-start.22
  66.0 4.9 %collective-permute-done.20.refs_1_ = bf16[64,1792]{1,0:T(8,128)(2,1)S(1)} collective-permute-done((bf16[64,1792]{1,0:T(8,128)(2,1)S(1)}, bf16[64,1792]{1,0:T(8,128)(2,1)S(1)}, u32[]{:S(2)}, u32[]{:S(2)}) %collective-permute-start.20) | collective-permute-done | bytes 229408 | tf_op jit(solution)/shard_map/ppermute | solution.py:50
  71.0 3.7 %collective-permute-done.21.refs_2_ = bf16[64,1792]{1,0:T(8,128)(2,1)S(1)} collective-permute-done((bf16[64,1792]{1,0:T(8,128)(2,1)S(1)}, bf16[64,1792]{1,0:T(8,128)(2,1)S(1)}, u32[]{:S(2)}, u32[]{:S(2)}) %collective-permute-start.21) | collective-permute-done | bytes 229408 | tf_op jit(solution)/shard_map/ppermute | solution.py:50
  74.6 1.6 %collective-permute-done.22.refs_3_ = bf16[64,1792]{1,0:T(8,128)(2,1)S(1)} collective-permute-done((bf16[64,1792]{1,0:T(8,128)(2,1)S(1)}, bf16[64,1792]{1,0:T(8,128)(2,1)S(1)}, u32[]{:S(2)}, u32[]{:S(2)}) %collective-permute-start.22) | collective-permute-done | bytes 229408 | tf_op jit(solution)/shard_map/ppermute | solution.py:50
  76.3 1.5 collective-permute-done.26.refs_7_
  77.7 11.6 %hidden_grads.1 = (bf16[8,64,896]{2,1,0:T(8,128)(2,1)S(1)}, bf16[2,32,608]{2,1,0:T(8,128)(2,1)S(1)}, bf16[2,32,608]{2,1,0:T(8,128)(2,1)S(1)}) custom-call(s32[9]{0:T(128)S(1)} %pad_add_fusion.place_ref, bf16[64,1792]{1,0:T(8,128)(2,1)S(1)} %constant_dynamic-update-slice_fusion.refs_0_, bf16[64,1792]{1,0:T(8,128)(2,1)S(1)} %collective-permute-done.20.refs_1_, ...), custom_call_target="tpu_custom_call" | custom-call | flops 557842432 | bytes 17432576 | tf_op jit(solution)/shard_map/hidden_grads/pallas_call | solution.py:260
  89.4 15.8 %backward.1 = (bf16[2,2,64,1792]{3,2,1,0:T(8,128)(2,1)S(1)}, bf16[2,2,64,1792]{3,2,1,0:T(8,128)(2,1)S(1)}) custom-call(s32[9]{0:T(128)S(1)} %pad_add_fusion.place_ref, bf16[2,32,608]{2,1,0:T(8,128)(2,1)S(1)} %get-tuple-element.29.dg_ref.refs_0_, bf16[2,32,608]{2,1,0:T(8,128)(2,1)S(1)} %get-tuple-element.30.du_ref.refs_1_, ...), custom_call_target="tpu_custom_call" | custom-call | flops 1115684864 | bytes 34865152 | tf_op jit(solution)/shard_map/backward/pallas_call | solution.py:260
  105.2 0.2 collective-permute-start.27
  105.4 9.6 %grad_down.1 = bf16[2,608,7168]{2,1,0:T(8,128)(2,1)} custom-call(s32[9]{0:T(128)S(1)} %pad_add_fusion.place_ref, bf16[2,32,608]{2,1,0:T(8,128)(2,1)S(1)} %get-tuple-element.21.act_ref.refs_0_, bf16[8,64,896]{2,1,0:T(8,128)(2,1)S(1)} %get-tuple-element.36.refs_1_), custom_call_target="tpu_custom_call" | custom-call | flops 557842432 | bytes 17432576 | tf_op jit(solution)/shard_map/grad_down/pallas_call | solution.py:260
  115.0 13.9 %grad_gate_up.1 = (bf16[2,608,7168]{2,1,0:T(8,128)(2,1)}, bf16[2,608,7168]{2,1,0:T(8,128)(2,1)}) custom-call(s32[9]{0:T(128)S(1)} %pad_add_fusion.place_ref, bf16[2,32,608]{2,1,0:T(8,128)(2,1)S(1)} %get-tuple-element.29.dg_ref.refs_0_, bf16[2,32,608]{2,1,0:T(8,128)(2,1)S(1)} %get-tuple-element.30.du_ref.refs_1_, ...), custom_call_target="tpu_custom_call" | custom-call | flops 1115684864 | bytes 34865152 | tf_op jit(solution)/shard_map/grad_gate_up/pallas_call | solution.py:260
  128.9 0.2 add_convert_fusion.1
  129.1 2.2 %collective-permute-start.13 = (bf16[64,1792]{1,0:T(8,128)(2,1)S(1)}, bf16[64,1792]{1,0:T(8,128)(2,1)S(1)}, u32[]{:S(2)}, u32[]{:S(2)}) collective-permute-start(bf16[64,1792]{1,0:T(8,128)(2,1)S(1)} %get-tuple-element.41), channel_id=1, source_target_pairs={{0,6},{1,7},{2,4},{3,5},{4,2},{5,3},{6,0},{7,1},{8,14},{9,15},{10,... | collective-permute-start | bytes 688136 | tf_op jit(solution)/shard_map/ppermute | solution.py:50
  131.3 0.5 collective-permute-start.12
  131.9 0.8 collective-permute-start.11
  132.7 0.2 add_convert_fusion
  133.0 2.2 %collective-permute-start.30 = (bf16[64,1792]{1,0:T(8,128)(2,1)S(1)}, bf16[64,1792]{1,0:T(8,128)(2,1)S(1)}, u32[]{:S(2)}, u32[]{:S(2)}) collective-permute-start(bf16[64,1792]{1,0:T(8,128)(2,1)S(1)} %get-tuple-element.38), channel_id=1, source_target_pairs={{0,6},{1,7},{2,4},{3,5},{4,2},{5,3},{6,0},{7,1},{8,14},{9,15},{10,... | collective-permute-start | bytes 688136 | tf_op jit(solution)/shard_map/ppermute | solution.py:50
  135.2 0.5 collective-permute-start.29
  135.7 2.9 %collective-permute-done.13 = bf16[64,1792]{1,0:T(8,128)(2,1)S(1)} collective-permute-done((bf16[64,1792]{1,0:T(8,128)(2,1)S(1)}, bf16[64,1792]{1,0:T(8,128)(2,1)S(1)}, u32[]{:S(2)}, u32[]{:S(2)}) %collective-permute-start.13) | collective-permute-done | bytes 229408 | tf_op jit(solution)/shard_map/ppermute | solution.py:50
  138.6 1.2 collective-permute-start.28
  139.8 3.5 %collective-permute-done.12 = bf16[64,1792]{1,0:T(8,128)(2,1)S(1)} collective-permute-done((bf16[64,1792]{1,0:T(8,128)(2,1)S(1)}, bf16[64,1792]{1,0:T(8,128)(2,1)S(1)}, u32[]{:S(2)}, u32[]{:S(2)}) %collective-permute-start.12) | collective-permute-done | bytes 229408 | tf_op jit(solution)/shard_map/ppermute | solution.py:50
  143.2 0.3 collective-permute-done.11
  143.6 0.1 fusion.5
  143.7 0.8 collective-permute-start.16
  144.6 3.9 %collective-permute-done.30 = bf16[64,1792]{1,0:T(8,128)(2,1)S(1)} collective-permute-done((bf16[64,1792]{1,0:T(8,128)(2,1)S(1)}, bf16[64,1792]{1,0:T(8,128)(2,1)S(1)}, u32[]{:S(2)}, u32[]{:S(2)}) %collective-permute-start.30) | collective-permute-done | bytes 229408 | tf_op jit(solution)/shard_map/ppermute | solution.py:50
  148.5 0.1 collective-permute-start.14
  148.6 3.9 %collective-permute-done.29 = bf16[64,1792]{1,0:T(8,128)(2,1)S(1)} collective-permute-done((bf16[64,1792]{1,0:T(8,128)(2,1)S(1)}, bf16[64,1792]{1,0:T(8,128)(2,1)S(1)}, u32[]{:S(2)}, u32[]{:S(2)}) %collective-permute-start.29) | collective-permute-done | bytes 229408 | tf_op jit(solution)/shard_map/ppermute | solution.py:50
  152.5 0.2 collective-permute-done.28
  152.7 0.1 fusion.2
  152.9 0.8 collective-permute-start.33
  153.7 3.0 %collective-permute-start.31 = (bf16[16,1792]{1,0:T(8,128)(2,1)S(1)}, bf16[16,1792]{1,0:T(8,128)(2,1)S(1)}, u32[]{:S(2)}, u32[]{:S(2)}) collective-permute-start(bf16[16,1792]{1,0:T(8,128)(2,1)S(1)} %get-tuple-element.43), channel_id=1, source_target_pairs={{0,24},{1,25},{2,26},{3,27},{4,28},{5,29},{6,30},{7,31},{8,0},{9,1... | collective-permute-start | bytes 172040 | tf_op jit(solution)/shard_map/ppermute | solution.py:50
  156.8 0.7 add_convert_fusion.3
  157.4 2.2 %collective-permute-done.33 = bf16[16,1792]{1,0:T(8,128)(2,1)S(1)} collective-permute-done((bf16[16,1792]{1,0:T(8,128)(2,1)S(1)}, bf16[16,1792]{1,0:T(8,128)(2,1)S(1)}, u32[]{:S(2)}, u32[]{:S(2)}) %collective-permute-start.33) | collective-permute-done | bytes 57376 | tf_op jit(solution)/shard_map/ppermute | solution.py:50
  159.6 1.6 collective-permute-done.32
  161.2 0.7 add_convert_fusion.2
  (35 shorter events, 0.2 us)
Async XLA Ops:
  3.9 9.4 %collective-permute-start.2 = (bf16[16,1920]{1,0:T(8,128)(2,1)S(1)}, bf16[16,1920]{1,0:T(8,128)(2,1)S(1)}, u32[]{:S(2)}, u32[]{:S(2)}) collective-permute-start(bf16[16,1920]{1,0:T(8,128)(2,1)S(1)} %pad_maximum_fusion.1), channel_id=1, source_target_pairs={{0,24},{1,25},{2,26},{3,27},{4,28},{5,29},{6,30},{7,31},{8,0},{9,1... | collective-permute-start | bytes 184328 | tf_op jit(solution)/shard_map/ppermute | solution.py:50
  8.9 9.1 %collective-permute-start.1 = (bf16[16,1920]{1,0:T(8,128)(2,1)S(1)}, bf16[16,1920]{1,0:T(8,128)(2,1)S(1)}, u32[]{:S(2)}, u32[]{:S(2)}) collective-permute-start(bf16[16,1920]{1,0:T(8,128)(2,1)S(1)} %pad_maximum_fusion.1), channel_id=1, source_target_pairs={{0,16},{1,17},{2,18},{3,19},{4,20},{5,21},{6,22},{7,23},{8,24},{9,... | collective-permute-start | bytes 184328 | tf_op jit(solution)/shard_map/ppermute | solution.py:50
  8.9 9.1 %collective-permute-start = (bf16[16,1920]{1,0:T(8,128)(2,1)S(1)}, bf16[16,1920]{1,0:T(8,128)(2,1)S(1)}, u32[]{:S(2)}, u32[]{:S(2)}) collective-permute-start(bf16[16,1920]{1,0:T(8,128)(2,1)S(1)} %pad_maximum_fusion.1), channel_id=1, source_target_pairs={{0,8},{1,9},{2,10},{3,11},{4,12},{5,13},{6,14},{7,15},{8,16},{9,17... | collective-permute-start | bytes 184328 | tf_op jit(solution)/shard_map/ppermute | solution.py:50
  9.9 13.4 %collective-permute-start.17 = (bf16[16,1792]{1,0:T(8,128)(2,1)}, bf16[16,1792]{1,0:T(8,128)(2,1)S(1)}, u32[]{:S(2)}, u32[]{:S(2)}) collective-permute-start(bf16[16,1792]{1,0:T(8,128)(2,1)} %param.8), channel_id=1, source_target_pairs={{0,8},{1,9},{2,10},{3,11},{4,12},{5,13},{6,14},{7,15},{8,16},{9,17... | collective-permute-start | bytes 172040 | tf_op jit(solution)/shard_map/ppermute | solution.py:50
  12.4 19.8 %collective-permute-start.18 = (bf16[16,1792]{1,0:T(8,128)(2,1)}, bf16[16,1792]{1,0:T(8,128)(2,1)S(1)}, u32[]{:S(2)}, u32[]{:S(2)}) collective-permute-start(bf16[16,1792]{1,0:T(8,128)(2,1)} %param.8), channel_id=1, source_target_pairs={{0,16},{1,17},{2,18},{3,19},{4,20},{5,21},{6,22},{7,23},{8,24},{9,... | collective-permute-start | bytes 172040 | tf_op jit(solution)/shard_map/ppermute | solution.py:50
  18.8 9.0 %collective-permute-start.3 = (bf16[64,1920]{1,0:T(8,128)(2,1)S(1)}, bf16[64,1920]{1,0:T(8,128)(2,1)S(1)}, u32[]{:S(2)}, u32[]{:S(2)}) collective-permute-start(bf16[64,1920]{1,0:T(8,128)(2,1)S(1)} %pad_maximum_fusion.refs_0_), channel_id=1, source_target_pairs={{0,4},{1,5},{2,6},{3,7},{4,0},{5,1},{6,2},{7,3},{8,12},{9,13},{10,... | collective-permute-start | bytes 737288 | tf_op jit(solution)/shard_map/ppermute | solution.py:50
  20.4 11.3 %collective-permute-start.4 = (bf16[64,1920]{1,0:T(8,128)(2,1)S(1)}, bf16[64,1920]{1,0:T(8,128)(2,1)S(1)}, u32[]{:S(2)}, u32[]{:S(2)}) collective-permute-start(bf16[64,1920]{1,0:T(8,128)(2,1)S(1)} %pad_maximum_fusion.refs_0_), channel_id=1, source_target_pairs={{0,2},{1,3},{2,0},{3,1},{4,6},{5,7},{6,4},{7,5},{8,10},{9,11},{10,... | collective-permute-start | bytes 737288 | tf_op jit(solution)/shard_map/ppermute | solution.py:50
  21.9 9.8 %collective-permute-start.5 = (bf16[64,1920]{1,0:T(8,128)(2,1)S(1)}, bf16[64,1920]{1,0:T(8,128)(2,1)S(1)}, u32[]{:S(2)}, u32[]{:S(2)}) collective-permute-start(bf16[64,1920]{1,0:T(8,128)(2,1)S(1)} %pad_maximum_fusion.refs_0_), channel_id=1, source_target_pairs={{0,6},{1,7},{2,4},{3,5},{4,2},{5,3},{6,0},{7,1},{8,14},{9,15},{10,... | collective-permute-start | bytes 737288 | tf_op jit(solution)/shard_map/ppermute | solution.py:50
  23.3 9.0 %collective-permute-start.6 = (bf16[64,1920]{1,0:T(8,128)(2,1)S(1)}, bf16[64,1920]{1,0:T(8,128)(2,1)S(1)}, u32[]{:S(2)}, u32[]{:S(2)}) collective-permute-start(bf16[64,1920]{1,0:T(8,128)(2,1)S(1)} %pad_maximum_fusion.refs_0_), channel_id=1, source_target_pairs={{0,1},{1,0},{2,3},{3,2},{4,5},{5,4},{6,7},{7,6},{8,9},{9,8},{10,11... | collective-permute-start | bytes 737288 | tf_op jit(solution)/shard_map/ppermute | solution.py:50
  27.8 4.5 %collective-permute-start.7 = (bf16[64,1920]{1,0:T(8,128)(2,1)S(1)}, bf16[64,1920]{1,0:T(8,128)(2,1)S(1)}, u32[]{:S(2)}, u32[]{:S(2)}) collective-permute-start(bf16[64,1920]{1,0:T(8,128)(2,1)S(1)} %collective-permute-done.3.refs_1_), channel_id=1, source_target_pairs={{0,1},{1,0},{2,3},{3,2},{4,5},{5,4},{6,7},{7,6},{8,9},{9,8},{10,11... | collective-permute-start | bytes 737288 | tf_op jit(solution)/shard_map/ppermute | solution.py:50
  31.7 1.5 collective-permute-start.8
  31.7 1.9 %collective-permute-start.9 = (bf16[64,1920]{1,0:T(8,128)(2,1)S(1)}, bf16[64,1920]{1,0:T(8,128)(2,1)S(1)}, u32[]{:S(2)}, u32[]{:S(2)}) collective-permute-start(bf16[64,1920]{1,0:T(8,128)(2,1)S(1)} %collective-permute-done.5.refs_3_), channel_id=1, source_target_pairs={{0,1},{1,0},{2,3},{3,2},{4,5},{5,4},{6,7},{7,6},{8,9},{9,8},{10,11... | collective-permute-start | bytes 737288 | tf_op jit(solution)/shard_map/ppermute | solution.py:50
  32.2 30.2 %collective-permute-start.19 = (bf16[16,1792]{1,0:T(8,128)(2,1)}, bf16[16,1792]{1,0:T(8,128)(2,1)S(1)}, u32[]{:S(2)}, u32[]{:S(2)}) collective-permute-start(bf16[16,1792]{1,0:T(8,128)(2,1)} %param.8), channel_id=1, source_target_pairs={{0,24},{1,25},{2,26},{3,27},{4,28},{5,29},{6,30},{7,31},{8,0},{9,1... | collective-permute-start | bytes 172040 | tf_op jit(solution)/shard_map/ppermute | solution.py:50
  62.2 66.6 %collective-permute-start.10 = (bf16[2,2,64,1792]{3,2,1,0:T(8,128)(2,1)S(1)}, bf16[2,2,64,1792]{3,2,1,0:T(8,128)(2,1)S(1)}, u32[]{:S(2)}, u32[]{:S(2)}) collective-permute-start(bf16[2,2,64,1792]{3,2,1,0:T(8,128)(2,1)S(1)} %get-tuple-element.25), channel_id=1, source_target_pairs={{0,1},{1,0},{2,3},{3,2},{4,5},{5,4},{6,7},{7,6},{8,9},{9,8},{10,11... | collective-permute-start | bytes 2752520 | tf_op jit(solution)/shard_map/ppermute | solution.py:50
  62.5 8.5 %collective-permute-start.20 = (bf16[64,1792]{1,0:T(8,128)(2,1)S(1)}, bf16[64,1792]{1,0:T(8,128)(2,1)S(1)}, u32[]{:S(2)}, u32[]{:S(2)}) collective-permute-start(bf16[64,1792]{1,0:T(8,128)(2,1)S(1)} %constant_dynamic-update-slice_fusion.refs_0_), channel_id=1, source_target_pairs={{0,4},{1,5},{2,6},{3,7},{4,0},{5,1},{6,2},{7,3},{8,12},{9,13},{10,... | collective-permute-start | bytes 688136 | tf_op jit(solution)/shard_map/ppermute | solution.py:50
  63.4 11.2 %collective-permute-start.21 = (bf16[64,1792]{1,0:T(8,128)(2,1)S(1)}, bf16[64,1792]{1,0:T(8,128)(2,1)S(1)}, u32[]{:S(2)}, u32[]{:S(2)}) collective-permute-start(bf16[64,1792]{1,0:T(8,128)(2,1)S(1)} %constant_dynamic-update-slice_fusion.refs_0_), channel_id=1, source_target_pairs={{0,2},{1,3},{2,0},{3,1},{4,6},{5,7},{6,4},{7,5},{8,10},{9,11},{10,... | collective-permute-start | bytes 688136 | tf_op jit(solution)/shard_map/ppermute | solution.py:50
  64.6 11.7 %collective-permute-start.22 = (bf16[64,1792]{1,0:T(8,128)(2,1)S(1)}, bf16[64,1792]{1,0:T(8,128)(2,1)S(1)}, u32[]{:S(2)}, u32[]{:S(2)}) collective-permute-start(bf16[64,1792]{1,0:T(8,128)(2,1)S(1)} %constant_dynamic-update-slice_fusion.refs_0_), channel_id=1, source_target_pairs={{0,6},{1,7},{2,4},{3,5},{4,2},{5,3},{6,0},{7,1},{8,14},{9,15},{10,... | collective-permute-start | bytes 688136 | tf_op jit(solution)/shard_map/ppermute | solution.py:50
  66.0 10.2 %collective-permute-start.23 = (bf16[64,1792]{1,0:T(8,128)(2,1)S(1)}, bf16[64,1792]{1,0:T(8,128)(2,1)S(1)}, u32[]{:S(2)}, u32[]{:S(2)}) collective-permute-start(bf16[64,1792]{1,0:T(8,128)(2,1)S(1)} %constant_dynamic-update-slice_fusion.refs_0_), channel_id=1, source_target_pairs={{0,1},{1,0},{2,3},{3,2},{4,5},{5,4},{6,7},{7,6},{8,9},{9,8},{10,11... | collective-permute-start | bytes 688136 | tf_op jit(solution)/shard_map/ppermute | solution.py:50
  70.9 5.3 %collective-permute-start.24 = (bf16[64,1792]{1,0:T(8,128)(2,1)S(1)}, bf16[64,1792]{1,0:T(8,128)(2,1)S(1)}, u32[]{:S(2)}, u32[]{:S(2)}) collective-permute-start(bf16[64,1792]{1,0:T(8,128)(2,1)S(1)} %collective-permute-done.20.refs_1_), channel_id=1, source_target_pairs={{0,1},{1,0},{2,3},{3,2},{4,5},{5,4},{6,7},{7,6},{8,9},{9,8},{10,11... | collective-permute-start | bytes 688136 | tf_op jit(solution)/shard_map/ppermute | solution.py:50
  74.6 1.6 %collective-permute-start.25 = (bf16[64,1792]{1,0:T(8,128)(2,1)S(1)}, bf16[64,1792]{1,0:T(8,128)(2,1)S(1)}, u32[]{:S(2)}, u32[]{:S(2)}) collective-permute-start(bf16[64,1792]{1,0:T(8,128)(2,1)S(1)} %collective-permute-done.21.refs_2_), channel_id=1, source_target_pairs={{0,1},{1,0},{2,3},{3,2},{4,5},{5,4},{6,7},{7,6},{8,9},{9,8},{10,11... | collective-permute-start | bytes 688136 | tf_op jit(solution)/shard_map/ppermute | solution.py:50
  76.3 1.5 collective-permute-start.26
  105.2 27.6 %collective-permute-start.27 = (bf16[2,2,64,1792]{3,2,1,0:T(8,128)(2,1)S(1)}, bf16[2,2,64,1792]{3,2,1,0:T(8,128)(2,1)S(1)}, u32[]{:S(2)}, u32[]{:S(2)}) collective-permute-start(bf16[2,2,64,1792]{3,2,1,0:T(8,128)(2,1)S(1)} %get-tuple-element.32), channel_id=1, source_target_pairs={{0,1},{1,0},{2,3},{3,2},{4,5},{5,4},{6,7},{7,6},{8,9},{9,8},{10,11... | collective-permute-start | bytes 2752520 | tf_op jit(solution)/shard_map/ppermute | solution.py:50
  129.1 9.4 %collective-permute-start.13 = (bf16[64,1792]{1,0:T(8,128)(2,1)S(1)}, bf16[64,1792]{1,0:T(8,128)(2,1)S(1)}, u32[]{:S(2)}, u32[]{:S(2)}) collective-permute-start(bf16[64,1792]{1,0:T(8,128)(2,1)S(1)} %get-tuple-element.41), channel_id=1, source_target_pairs={{0,6},{1,7},{2,4},{3,5},{4,2},{5,3},{6,0},{7,1},{8,14},{9,15},{10,... | collective-permute-start | bytes 688136 | tf_op jit(solution)/shard_map/ppermute | solution.py:50
  131.3 11.9 %collective-permute-start.12 = (bf16[64,1792]{1,0:T(8,128)(2,1)S(1)}, bf16[64,1792]{1,0:T(8,128)(2,1)S(1)}, u32[]{:S(2)}, u32[]{:S(2)}) collective-permute-start(bf16[64,1792]{1,0:T(8,128)(2,1)S(1)} %get-tuple-element.42), channel_id=1, source_target_pairs={{0,4},{1,5},{2,6},{3,7},{4,0},{5,1},{6,2},{7,3},{8,12},{9,13},{10,... | collective-permute-start | bytes 688136 | tf_op jit(solution)/shard_map/ppermute | solution.py:50
  131.9 11.7 %collective-permute-start.11 = (bf16[64,1792]{1,0:T(8,128)(2,1)S(1)}, bf16[64,1792]{1,0:T(8,128)(2,1)S(1)}, u32[]{:S(2)}, u32[]{:S(2)}) collective-permute-start(bf16[64,1792]{1,0:T(8,128)(2,1)S(1)} %get-tuple-element.40), channel_id=1, source_target_pairs={{0,2},{1,3},{2,0},{3,1},{4,6},{5,7},{6,4},{7,5},{8,10},{9,11},{10,... | collective-permute-start | bytes 688136 | tf_op jit(solution)/shard_map/ppermute | solution.py:50
  133.0 15.5 %collective-permute-start.30 = (bf16[64,1792]{1,0:T(8,128)(2,1)S(1)}, bf16[64,1792]{1,0:T(8,128)(2,1)S(1)}, u32[]{:S(2)}, u32[]{:S(2)}) collective-permute-start(bf16[64,1792]{1,0:T(8,128)(2,1)S(1)} %get-tuple-element.38), channel_id=1, source_target_pairs={{0,6},{1,7},{2,4},{3,5},{4,2},{5,3},{6,0},{7,1},{8,14},{9,15},{10,... | collective-permute-start | bytes 688136 | tf_op jit(solution)/shard_map/ppermute | solution.py:50
  135.2 17.3 %collective-permute-start.29 = (bf16[64,1792]{1,0:T(8,128)(2,1)S(1)}, bf16[64,1792]{1,0:T(8,128)(2,1)S(1)}, u32[]{:S(2)}, u32[]{:S(2)}) collective-permute-start(bf16[64,1792]{1,0:T(8,128)(2,1)S(1)} %get-tuple-element.39), channel_id=1, source_target_pairs={{0,4},{1,5},{2,6},{3,7},{4,0},{5,1},{6,2},{7,3},{8,12},{9,13},{10,... | collective-permute-start | bytes 688136 | tf_op jit(solution)/shard_map/ppermute | solution.py:50
  138.6 14.2 %collective-permute-start.28 = (bf16[64,1792]{1,0:T(8,128)(2,1)S(1)}, bf16[64,1792]{1,0:T(8,128)(2,1)S(1)}, u32[]{:S(2)}, u32[]{:S(2)}) collective-permute-start(bf16[64,1792]{1,0:T(8,128)(2,1)S(1)} %get-tuple-element.37), channel_id=1, source_target_pairs={{0,2},{1,3},{2,0},{3,1},{4,6},{5,7},{6,4},{7,5},{8,10},{9,11},{10,... | collective-permute-start | bytes 688136 | tf_op jit(solution)/shard_map/ppermute | solution.py:50
  143.7 10.0 %collective-permute-start.16 = (bf16[16,1792]{1,0:T(8,128)(2,1)S(1)}, bf16[16,1792]{1,0:T(8,128)(2,1)S(1)}, u32[]{:S(2)}, u32[]{:S(2)}) collective-permute-start(bf16[16,1792]{1,0:T(8,128)(2,1)S(1)} %get-tuple-element.47), channel_id=1, source_target_pairs={{0,8},{1,9},{2,10},{3,11},{4,12},{5,13},{6,14},{7,15},{8,16},{9,17... | collective-permute-start | bytes 172040 | tf_op jit(solution)/shard_map/ppermute | solution.py:50
  144.6 12.2 %collective-permute-start.15 = (bf16[16,1792]{1,0:T(8,128)(2,1)S(1)}, bf16[16,1792]{1,0:T(8,128)(2,1)S(1)}, u32[]{:S(2)}, u32[]{:S(2)}) collective-permute-start(bf16[16,1792]{1,0:T(8,128)(2,1)S(1)} %get-tuple-element.48), channel_id=1, source_target_pairs={{0,16},{1,17},{2,18},{3,19},{4,20},{5,21},{6,22},{7,23},{8,24},{9,... | collective-permute-start | bytes 172040 | tf_op jit(solution)/shard_map/ppermute | solution.py:50
  148.5 8.3 %collective-permute-start.14 = (bf16[16,1792]{1,0:T(8,128)(2,1)S(1)}, bf16[16,1792]{1,0:T(8,128)(2,1)S(1)}, u32[]{:S(2)}, u32[]{:S(2)}) collective-permute-start(bf16[16,1792]{1,0:T(8,128)(2,1)S(1)} %get-tuple-element.46), channel_id=1, source_target_pairs={{0,24},{1,25},{2,26},{3,27},{4,28},{5,29},{6,30},{7,31},{8,0},{9,1... | collective-permute-start | bytes 172040 | tf_op jit(solution)/shard_map/ppermute | solution.py:50
  152.9 6.7 %collective-permute-start.33 = (bf16[16,1792]{1,0:T(8,128)(2,1)S(1)}, bf16[16,1792]{1,0:T(8,128)(2,1)S(1)}, u32[]{:S(2)}, u32[]{:S(2)}) collective-permute-start(bf16[16,1792]{1,0:T(8,128)(2,1)S(1)} %get-tuple-element.44), channel_id=1, source_target_pairs={{0,8},{1,9},{2,10},{3,11},{4,12},{5,13},{6,14},{7,15},{8,16},{9,17... | collective-permute-start | bytes 172040 | tf_op jit(solution)/shard_map/ppermute | solution.py:50
  153.7 7.4 %collective-permute-start.32 = (bf16[16,1792]{1,0:T(8,128)(2,1)S(1)}, bf16[16,1792]{1,0:T(8,128)(2,1)S(1)}, u32[]{:S(2)}, u32[]{:S(2)}) collective-permute-start(bf16[16,1792]{1,0:T(8,128)(2,1)S(1)} %get-tuple-element.45), channel_id=1, source_target_pairs={{0,16},{1,17},{2,18},{3,19},{4,20},{5,21},{6,22},{7,23},{8,24},{9,... | collective-permute-start | bytes 172040 | tf_op jit(solution)/shard_map/ppermute | solution.py:50
  153.7 7.4 %collective-permute-start.31 = (bf16[16,1792]{1,0:T(8,128)(2,1)S(1)}, bf16[16,1792]{1,0:T(8,128)(2,1)S(1)}, u32[]{:S(2)}, u32[]{:S(2)}) collective-permute-start(bf16[16,1792]{1,0:T(8,128)(2,1)S(1)} %get-tuple-element.43), channel_id=1, source_target_pairs={{0,24},{1,25},{2,26},{3,27},{4,28},{5,29},{6,30},{7,31},{8,0},{9,1... | collective-permute-start | bytes 172040 | tf_op jit(solution)/shard_map/ppermute | solution.py:50

commit v2 on v0

v2 whole, which is shorter than its diff:
```python
import functools
import math

import jax
import jax.numpy as jnp
from jax import lax
from jax.experimental import pallas as pl
from jax.experimental.pallas import tpu as pltpu
from jax.sharding import PartitionSpec as P

CAP = 4
LANES = 128
MIB = 1 << 20
MFLOP = 10**6
F32 = jnp.float32
BF16 = jnp.bfloat16
AXES = ("dp", "hst")


def dot(a, b):
    return lax.dot_general(a, b, (((1,), (0,)), ((), ())), preferred_element_type=F32)


def dot_t(a, b):
    return lax.dot_general(a, b, (((1,), (1,)), ((), ())), preferred_element_type=F32)


def log2(n):
    assert n & (n - 1) == 0
    return n.bit_length() - 1


class Grid:
    def __init__(self, dp, hst):
        self.dp, self.hst = dp, hst
        self.nc = 2 if hst % 2 == 0 else 1
        self.ny = hst // self.nc
        self.nx = self.ny if dp % self.ny == 0 else 1
        self.nz = dp // self.nx
        assert self.nz & (self.nz - 1) == 0
        self.square = [(a, b) for a in range(self.nx) for b in range(self.ny)]

    def shift(self, value, dz=0, dx=0, dy=0, dc=0):
        pairs = []
        for z in range(self.nz):
            for x in range(self.nx):
                for y in range(self.ny):
                    for c in range(self.nc):
                        to_dp = (z ^ dz) * self.nx + (x + dx) % self.nx
                        to_hst = (y + dy) % self.ny * self.nc + (c + dc) % self.nc
                        here = (z * self.nx + x) * self.hst + y * self.nc + c
                        pairs.append((here, to_dp * self.hst + to_hst))
        return lax.ppermute(value, AXES, pairs)

    def along_z(self, mine):
        return [mine] + [self.shift(mine, dz=k) for k in range(1, self.nz)]

    def doubled_along_z(self, mine):
        column, k = mine, 1
        while k < self.nz:
            column = stack([column, self.shift(column, dz=k)], [], "double")
            k *= 2
        return column

    def over_plane(self, column):
        return {(a, b): self.shift(column, dx=a, dy=b) if a or b else column for a, b in self.square}

    def over_cores(self, plane):
        planes = [plane]
        for c in range(1, self.nc):
            planes.append({at: self.shift(block, dc=c) for at, block in plane.items()})
        return [p[a, b] for p in planes for b in range(self.ny) for a in range(self.nx)]

    def source(self, k):
        host = lax.axis_index("hst")
        y, core = host >> log2(self.nc), host & (self.nc - 1)
        return (((y - k % self.ny) & (self.ny - 1)) << log2(self.nc)) + ((core + k // self.ny) & (self.nc - 1))


def call(kernel, name, outs, args, specs=None, out_specs=None, scratch=(), grid=(), limit=16, cost=0):
    specs = specs or [pl.BlockSpec(memory_space=pltpu.VMEM)] * len(args)
    out_specs = out_specs or [pl.BlockSpec(memory_space=pltpu.VMEM)] * len(outs)
    return pl.pallas_call(
        kernel,
        name=name,
        grid=grid,
        out_shape=outs,
        in_specs=specs,
        out_specs=out_specs,
        scratch_shapes=list(scratch),
        compiler_params=pltpu.CompilerParams(vmem_limit_bytes=limit * MIB),
        cost_estimate=pl.CostEstimate(flops=cost * MFLOP, bytes_accessed=0, transcendentals=0),
    )(*args)


def shaped(dtype, *dims):
    return jax.ShapeDtypeStruct(dims, dtype)


VECTORS = pl.BlockSpec(memory_space=pltpu.VMEM)
ANYWHERE = pl.BlockSpec(memory_space=pl.ANY)


def hold_kernel(source, _, held, sems):
    local, pieces = sems.shape
    part = source.shape[1] // pieces
    copies = []
    for e in range(local):
        for k in range(pieces):
            at = (e, pl.ds(k * part, part))
            copies.append(pltpu.make_async_copy(source.at[at], held.at[at], sems.at[e, k]))
    for copy in copies:
        copy.start()
    for copy in copies:
        copy.wait()


def hold(weight, after, name):
    pieces = 2 if weight.shape[1] % 32 == 0 else 1
    (held,) = call(
        hold_kernel,
        name,
        [pltpu.VMEM(weight.shape, BF16)],
        [hbm(weight), after],
        specs=[ANYWHERE] * 2,
        scratch=[pltpu.SemaphoreType.DMA((weight.shape[0], pieces))],
        cost=12000,
    )
    return held


def hbm(weight):
    return pltpu.with_memory_space_constraint(weight, pltpu.HBM)


def pack_kernel(tokens_ref, ids_ref, gates_ref, out_ref):
    rows, width = tokens_ref.shape
    out_ref[:, :width] = tokens_ref[...]
    gates = gates_ref[...]
    high = gates.astype(BF16).astype(F32)
    middle = (gates - high).astype(BF16).astype(F32)
    low = gates - high - middle
    lane = lax.broadcasted_iota(jnp.int32, (rows, LANES), 1)
    aux = jnp.zeros((rows, LANES), F32)
    for k, part in enumerate([ids_ref[...].astype(F32), high, middle, low]):
        for n in range(2):
            aux = jnp.where(lane == 2 * k + n, part[:, n : n + 1], aux)
    out_ref[:, width:] = aux.astype(BF16)


def stack_kernel(count, later, *refs):
    parts, out_ref = refs[:count], refs[-1 - later]
    rows = parts[0].shape[0]
    for k, part in enumerate(parts):
        out_ref[k * rows : (k + 1) * rows] = part[...]
    if later:
        refs[-1][...] = refs[count][...]


def stack(parts, after, name, later=()):
    rows, width = parts[0].shape
    outs = call(
        functools.partial(stack_kernel, len(parts), len(later)),
        name,
        [shaped(BF16, rows * len(parts), width)] + [shaped(BF16, *array.shape) for array in later],
        [*parts, *later, *after],
        specs=[VECTORS] * (len(parts) + len(later)) + [ANYWHERE] * len(after),
        limit=16,
    )
    return outs if later else outs[0]


def add_kernel(count, skip, *refs):
    parts, outs = refs[:count], refs[count + skip :]
    total = parts[0][...].astype(F32)
    for part in parts[1:]:
        total = total + part[...].astype(F32)
    total = total.astype(BF16).reshape((len(outs),) + outs[0].shape)
    for k, out in enumerate(outs):
        out[...] = total[k]


def add(parts, pieces, after, name):
    *lead, rows, width = parts[0].shape
    each = math.prod(lead) * rows // pieces
    return call(
        functools.partial(add_kernel, len(parts), len(after)),
        name,
        [shaped(BF16, each, width)] * pieces,
        [*parts, *after],
        specs=[VECTORS] * len(parts) + [ANYWHERE] * len(after),
        limit=16,
    )


def back_over_cores(grid, parts, after, name):
    got = [grid.shift(parts[c], dc=-c) for c in range(1, grid.nc)]
    return add([parts[0], *got], len(grid.square), after, name)


def back_over_plane(grid, kept, after, name):
    got = [grid.shift(part, dx=-a, dy=-b) for part, (a, b) in zip(kept[1:], grid.square[1:])]
    return add([kept[0], *got], grid.nz, after, name)


def back_along_z(grid, total, after, name):
    got = [grid.shift(total[k], dz=k) for k in range(1, grid.nz)]
    return add([total[0], *got], 1, after, name)[0]


def tables(aux, first, rows, local, block):
    tokens = aux.shape[0]
    across = jnp.transpose(aux.astype(F32))
    ids = [across[k : k + 1] for k in range(2)]
    gates = [across[2 + k : 3 + k] + across[4 + k : 5 + k] + across[6 + k : 7 + k] for k in range(2)]
    total = local * rows
    r = lax.broadcasted_iota(jnp.int32, (total, tokens), 0)
    j = lax.broadcasted_iota(jnp.int32, (total, tokens), 1)
    expert = ((r >> log2(rows)) + first).astype(F32)
    own_block = ((r & (rows - 1)) >> log2(CAP)) == (j >> log2(block))
    slot = (r & (CAP - 1)).astype(F32)
    hits = [(ids[k] == expert).astype(F32) for k in range(2)]
    hit = hits[0] + hits[1]
    up = lax.broadcasted_iota(jnp.int32, (tokens, tokens), 0)
    to = lax.broadcasted_iota(jnp.int32, (tokens, tokens), 1)
    earlier = ((up >> log2(block)) == (to >> log2(block))) & (up < to)
    position = dot(hit.astype(BF16), jnp.where(earlier, 1.0, 0.0).astype(BF16))
    select = jnp.where(own_block & (position == slot), hit, 0.0)
    gate = jnp.sum(select * (hits[0] * gates[0] + hits[1] * gates[1]), axis=1, keepdims=True)
    return select, gate


def streamed(weight, held, sems, starts):
    depth, width = held.shape[0], held.shape[-1]
    copies = [
        pltpu.make_async_copy(weight.at[:, :, pl.ds(start, width)], held.at[k % depth], sems.at[k % depth])
        for k, start in enumerate(starts)
    ]
    for copy in copies[:depth]:
        copy.start()

    def each():
        for k, copy in enumerate(copies):
            copy.wait()
            yield k, held.at[k % depth]
            if k + depth < len(copies):
                copies[k + depth].start()

    return each()


class Sizes:
    def __init__(self, grid, tokens, w_gate):
        self.grid = grid
        self.local, self.hidden, self.features = w_gate.shape
        self.block, self.width = tokens.shape
        self.rows = grid.dp * CAP
        self.total = self.local * self.rows
        self.count = grid.dp * self.block
        self.column = grid.nz * self.block
        self.blocks = grid.nc * grid.ny * grid.nx
        self.slices = grid.nc * grid.ny
        self.chunk = 896 if self.width % 896 == 0 else self.width
        self.per = self.width // self.chunk

    def relative_starts(self):
        return [
            pl.multiple_of(self.grid.source(k // self.per) * self.width + k % self.per * self.chunk, self.chunk)
            for k in range(self.slices * self.per)
        ]

    def at(self, e):
        return slice(e * self.rows, (e + 1) * self.rows)


def routed(s, blocks, select):
    for k in range(s.slices):
        group = blocks[k * s.grid.nx : (k + 1) * s.grid.nx]
        yield k, dot(select, jnp.concatenate([ref[:, : s.width] for ref in group], axis=0))


def gate_up_kernel(s, *refs):
    blocks = refs[: s.blocks]
    wg_ref, wu_ref, _, x_ref, select_ref, back_ref, gate_ref, act_ref, p_ref, q_ref, held, sems = refs[s.blocks :]
    chunks = streamed(wu_ref, held, sems, range(0, s.features, s.chunk))
    aux = jnp.concatenate([ref[:, s.width :] for ref in blocks[: s.grid.nx]], axis=0)
    select, gate = tables(aux, lax.axis_index("hst") * s.local, s.rows, s.local, s.block)
    gate_ref[...] = jnp.broadcast_to(gate, gate_ref.shape)
    select_ref[...] = select.astype(BF16)
    back_ref[...] = jnp.transpose(select).astype(BF16)
    for k, picked in routed(s, blocks, select.astype(BF16)):
        x_ref[s.grid.source(k)] = picked.astype(BF16)
    g, u = [0.0] * s.local, [0.0] * s.local
    for k, weight in chunks:
        at = k % s.per * s.chunk
        columns = slice(k * s.chunk, (k + 1) * s.chunk)
        for e in range(s.local):
            x = x_ref[k // s.per, s.at(e), at : at + s.chunk]
            g[e] += dot_t(x, wg_ref[e, :, columns])
            u[e] += dot_t(x, weight[e])
    for e in range(s.local):
        sigma = jax.nn.sigmoid(g[e])
        act_ref[e] = (g[e] * sigma * u[e]).astype(BF16)
        p_ref[e] = u[e] * sigma * (1.0 + g[e] * (1.0 - sigma))
        q_ref[e] = g[e] * sigma


def hidden_grads_kernel(s, *refs):
    blocks = refs[: s.blocks]
    select_ref, gate_ref, p_ref, q_ref, w_ref, d_ref, dg_ref, du_ref, held, sems = refs[s.blocks :]
    chunks = streamed(w_ref, held, sems, range(0, s.features, s.chunk))
    for k, picked in routed(s, blocks, select_ref[...]):
        d_ref[s.grid.source(k)] = (picked * gate_ref[:, :1]).astype(BF16)
    da = [0.0] * s.local
    for k, weight in chunks:
        at = k % s.per * s.chunk
        for e in range(s.local):
            da[e] += dot_t(d_ref[k // s.per, s.at(e), at : at + s.chunk], weight[e])
    for e in range(s.local):
        dg_ref[e] = (da[e] * p_ref[e]).astype(BF16)
        du_ref[e] = (da[e] * q_ref[e]).astype(BF16)


def to_tokens(s, k, at, found, back_ref, outs):
    each = s.slices // s.grid.nc
    sums = dot(back_ref[...], jnp.concatenate(found, axis=0)).astype(BF16)
    width = sums.shape[-1]
    outs[k // each][:, k % each, :, at : at + width] = sums.reshape(s.grid.nx, s.column, width)


def forward_kernel(s, act_ref, gate_ref, back_ref, w_ref, *refs):
    outs, (held, sems) = refs[:-2], refs[-2:]
    for k, weight in streamed(w_ref, held, sems, s.relative_starts()):
        found = [(dot(act_ref[e], weight[e]) * gate_ref[s.at(e), :1]).astype(BF16) for e in range(s.local)]
        to_tokens(s, k // s.per, k % s.per * s.chunk, found, back_ref, outs)


def backward_kernel(s, dg_ref, du_ref, back_ref, wg_ref, wu_ref, _, *refs):
    outs, (held, sems) = refs[:-2], refs[-2:]
    starts = s.relative_starts()
    for k, weight in streamed(wu_ref, held, sems, starts):
        columns = pl.ds(starts[k], s.chunk)
        found = [
            (dot(dg_ref[e], wg_ref[e, :, columns]) + dot(du_ref[e], weight[e])).astype(BF16)
            for e in range(s.local)
        ]
        to_tokens(s, k // s.per, k % s.per * s.chunk, found, back_ref, outs)


def grads_kernel(s, count, *refs):
    lefts, rows_ref = refs[:count], refs[count]
    outs, marker, turned = refs[count + 2 : 2 * count + 2], refs[2 * count + 2], refs[2 * count + 3 :]

    @pl.when(pl.program_id(0) == 0)
    def _():
        marker[...] = jnp.zeros_like(marker)
        for left, turn in zip(lefts, turned):
            for e in range(s.local):
                turn[e] = jnp.transpose(left[e].astype(F32)).astype(BF16)

    right = rows_ref[0]
    for turn, out in zip(turned, outs):
        for e in range(s.local):
            out[e] = dot(turn[e], right[s.at(e)]).astype(BF16)


def grads(s, name, lefts, right, after):
    chunk, per = s.chunk, s.per
    whole = pl.BlockSpec((s.local, s.rows, s.hidden), lambda i: (0, 0, 0))
    return call(
        functools.partial(grads_kernel, s, len(lefts)),
        name,
        [shaped(BF16, s.local, s.hidden, s.features)] * len(lefts) + [shaped(F32, 8, LANES)],
        [*lefts, right, after],
        specs=[whole] * len(lefts)
        + [pl.BlockSpec((1, s.total, chunk), lambda i: (i // per, 0, i % per)), ANYWHERE],
        out_specs=[pl.BlockSpec((s.local, s.hidden, chunk), lambda i: (0, 0, i))] * len(lefts)
        + [pl.BlockSpec((8, LANES), lambda i: (0, 0))],
        scratch=[pltpu.VMEM((s.local, s.hidden, s.rows), BF16)] * len(lefts),
        grid=(s.features // chunk,),
        limit=8 + 6 * len(lefts),
        cost=46000,
    )


def body(tokens, cotangent, expert_ids, gate_values, w_gate, w_up, w_down):
    grid = Grid(lax.axis_size("dp"), lax.axis_size("hst"))
    s = Sizes(grid, tokens, w_gate)

    (message,) = call(
        pack_kernel, "pack", [shaped(BF16, s.block, s.width + LANES)], [tokens, expert_ids, gate_values]
    )
    x_parts = grid.along_z(message)
    held_gate = hold(w_gate, message, "hold_gate")
    x_column, cotangent = stack(x_parts, [held_gate], "stack_tokens", [cotangent])
    x_plane = grid.over_plane(x_column)
    d_column = grid.doubled_along_z(cotangent)
    last = grid.square[-1]
    x_plane[last] = stack([x_plane[last]], [d_column], "relay")
    x_blocks = grid.over_cores(x_plane)
    d_column = stack([d_column], x_blocks, "stack_cotangents")
    streams = [pltpu.VMEM((3, s.local, s.hidden, s.chunk), BF16), pltpu.SemaphoreType.DMA((3,))]

    hidden_shape = (s.local, s.rows, s.hidden)
    rows_shape = shaped(BF16, s.slices, s.total, s.width)
    x_rows, select, back, gate, act, p, q = call(
        functools.partial(gate_up_kernel, s),
        "gate_up",
        [
            rows_shape,
            shaped(BF16, s.total, s.count),
            shaped(BF16, s.count, s.total),
            shaped(F32, s.total, LANES),
            shaped(BF16, *hidden_shape),
            shaped(F32, *hidden_shape),
            shaped(F32, *hidden_shape),
        ],
        [*x_blocks, held_gate, hbm(w_up), d_column],
        specs=[VECTORS] * (s.blocks + 1) + [ANYWHERE] * 2,
        scratch=streams,
        limit=16,
        cost=46000,
    )
    d_blocks = grid.over_cores(grid.over_plane(d_column))
    sums = shaped(BF16, grid.nx, grid.ny, s.column, s.width)
    out_parts = call(
        functools.partial(forward_kernel, s),
        "forward",
        [sums] * grid.nc,
        [act, gate, back, hbm(w_down)],
        specs=[VECTORS] * 3 + [ANYWHERE],
        scratch=streams,
        limit=16,
        cost=46000,
    )
    d_rows, d_gate, d_up = call(
        functools.partial(hidden_grads_kernel, s),
        "hidden_grads",
        [rows_shape, shaped(BF16, *hidden_shape), shaped(BF16, *hidden_shape)],
        [*d_blocks, select, gate, p, q, hbm(w_down)],
        specs=[VECTORS] * (s.blocks + 4) + [ANYWHERE],
        scratch=streams,
        limit=16,
        cost=46000,
    )
    mixed_kept = back_over_cores(grid, out_parts, [d_gate], "mixed_cores")
    back_parts = call(
        functools.partial(backward_kernel, s),
        "backward",
        [sums] * grid.nc,
        [d_gate, d_up, back, held_gate, hbm(w_up), mixed_kept[0]],
        specs=[VECTORS] * 4 + [ANYWHERE] * 2,
        scratch=streams,
        limit=16,
        cost=46000,
    )
    mixed_total = back_over_plane(grid, mixed_kept, back_parts[:1], "mixed_plane")
    grad_down, down_done = grads(s, "grad_down", [act], d_rows, mixed_total[0])
    mixed = back_along_z(grid, mixed_total, [down_done], "mixed_z")
    token_kept = back_over_cores(grid, back_parts, [down_done], "tokens_cores")
    grad_gate, grad_up, gate_up_done = grads(s, "grad_gate_up", [d_gate, d_up], x_rows, token_kept[0])
    token_total = back_over_plane(grid, token_kept, [gate_up_done], "tokens_plane")
    grad_tokens = back_along_z(grid, token_total, [], "tokens_z")
    return mixed, grad_tokens, grad_gate, grad_up, grad_down


def solution(mesh):
    return jax.shard_map(
        body,
        mesh=mesh,
        in_specs=(
            P("dp", "hst"),
            P("dp", "hst"),
            P("dp", None),
            P("dp", None),
            P("hst", "dp", None),
            P("hst", "dp", None),
            P("hst", "dp", None),
        ),
        out_specs=(
            P("dp", "hst"),
            P("dp", "hst"),
            P("hst", "dp", None),
            P("hst", "dp", None),
            P("hst", "dp", None),
        ),
        check_vma=False,
    )
```

time: 290 us -> 122 us (0.42)
  waiting for transfers between devices: 117 us -> 14.8 us
  matrix products: 79.7 us -> 0 us
  Pallas kernels: 0 us -> 69.1 us
  blocking collectives: 65.6 us -> 0 us
  starting transfers between devices: 7.9 us -> 34.6 us
  between operations: 14.6 us -> 0.88 us
    unnamed x4 -> x0, waiting for transfers between devices: 86.7 us -> none
    dot_general x13 -> x0, matrix products: 79.7 us -> none  [the longest x1 10.1 us: body(): jnp.einsum('erf,efd->erd', hidden, w_down, preferred_element_type=jnp.flo...]
    pallas_call x0 -> x19, Pallas kernels: none -> 69.1 us  [call(): pl.pallas_call(kernel, name=name, grid=grid, out_shape=outs, in_specs=spe...]
    all_gather x2 -> x0, blocking collectives: 65.6 us -> none  [the longest x1 33.4 us: body(): lax.all_gather(x_rows, 'dp', axis=1, tiled=True)]
    ppermute x0 -> x33, starting transfers between devices: none -> 34.6 us  [shift(): return lax.ppermute(value, AXES, pairs)]
    reduce_scatter x2 -> x0, waiting for transfers between devices: 23.3 us -> none  [the longest x1 22.9 us: body(): lax.psum_scatter(token_terms.astype(jnp.bfloat16), 'hst', scatter_dimensi...]
    ppermute x0 -> x33, waiting for transfers between devices: none -> 14.8 us  [shift(): return lax.ppermute(value, AXES, pairs)]
    all_to_all x2 -> x0, starting transfers between devices: 7.55 us -> none  [the longest x1 4.24 us: body(): lax.all_to_all(x_part, 'hst', split_axis=0, concat_axis=2, tiled=True)]
  transfers between devices with their start and end apart: 5 -> 33, of which waited for: 5 -> 9; matrix products, arithmetic and copies ran while one was open for 11% -> 0% of each run, Pallas kernels for 0% -> 56%
where the time goes in v2:
time: 122 us
  Pallas kernels  69.1 us (57%)
  starting transfers between devices  34.6 us (28%)
  waiting for transfers between devices  14.8 us (12%)
  local copies, waits for them, and re-layouts  2.34 us (2%)
    pallas_call x19, Pallas kernels, call(): pl.pallas_call(kernel, name=name, grid=grid, out_shape=outs, in_specs=spe...  69.1 us
    ppermute x33, starting transfers between devices, shift(): return lax.ppermute(value, AXES, pairs)  34.6 us
    ppermute x33, waiting for transfers between devices, shift(): return lax.ppermute(value, AXES, pairs)  14.8 us
  transfers between devices with their start and end apart: 33, of which 9 were waited for; matrix products, arithmetic and copies ran while one was open for 0% of the time, Pallas kernels for 56%

profile of v2, /device:TPU:0, one launch (start us, length us, event | category | flops | bytes accessed | tf_op | source)
XLA Modules:
  0.0 121.7 jit_solution(72169498296686568)
XLA Ops:
  0.6 0.8 copy.12.ids_ref
  1.4 0.8 copy.13.gates_ref
  2.1 0.8 copy-done
  3.0 0.1 pack.1._.refs_0_
  3.0 0.0 copy-start.1
  3.1 5.1 %collective-permute-start.2 = (bf16[16,1920]{1,0:T(8,128)(2,1)S(1)}, bf16[16,1920]{1,0:T(8,128)(2,1)S(1)}, u32[]{:S(2)}, u32[]{:S(2)}) collective-permute-start(bf16[16,1920]{1,0:T(8,128)(2,1)S(1)} %pack.1._.refs_0_), channel_id=1, source_target_pairs={{0,24},{1,25},{2,26},{3,27},{4,28},{5,29},{6,30},{7,31},{8,16},{9,... | collective-permute-start | bytes 184328 | tf_op jit(solution)/shard_map/ppermute | solution.py:53
  8.2 0.6 collective-permute-start
  8.8 6.1 %hold_gate.1.refs_5_.refs_8_.wg_ref = bf16[2,608,7168]{2,1,0:T(8,128)(2,1)S(1)} custom-call(bf16[2,608,7168]{2,1,0:T(8,128)(2,1)} %source.1, bf16[16,1920]{1,0:T(8,128)(2,1)S(1)} %pack.1._.refs_0_), custom_call_target="tpu_custom_call" | custom-call | flops 12000000000 | tf_op jit(solution)/shard_map/hold_gate/pallas_call | solution.py:83
  14.9 0.0 collective-permute-done.1.refs_2_
  14.9 0.0 collective-permute-done.refs_1_
  15.0 2.7 %collective-permute-start.5 = (bf16[64,1920]{1,0:T(8,128)(2,1)S(1)}, bf16[64,1920]{1,0:T(8,128)(2,1)S(1)}, u32[]{:S(2)}, u32[]{:S(2)}) collective-permute-start(bf16[64,1920]{1,0:T(8,128)(2,1)S(1)} %get-tuple-element.42.refs_1_.refs_0_), channel_id=1, source_target_pairs={{0,6},{1,7},{2,4},{3,5},{4,2},{5,3},{6,0},{7,1},{8,14},{9,15},{10,... | collective-permute-start | bytes 737288 | tf_op jit(solution)/shard_map/ppermute | solution.py:53
  17.6 0.5 collective-permute-start.4
  18.1 0.4 collective-permute-start.3
  18.5 1.4 %collective-permute-start.6 = (bf16[16,1792]{1,0:T(8,128)(2,1)S(1)}, bf16[16,1792]{1,0:T(8,128)(2,1)S(1)}, u32[]{:S(2)}, u32[]{:S(2)}) collective-permute-start(bf16[16,1792]{1,0:T(8,128)(2,1)S(1)} %get-tuple-element.43.refs_0_), channel_id=1, source_target_pairs={{0,8},{1,9},{2,10},{3,11},{4,12},{5,13},{6,14},{7,15},{8,0},{9,1},... | collective-permute-start | bytes 172040 | tf_op jit(solution)/shard_map/ppermute | solution.py:53
  19.9 2.8 %collective-permute-done.6.refs_1_ = bf16[16,1792]{1,0:T(8,128)(2,1)S(1)} collective-permute-done((bf16[16,1792]{1,0:T(8,128)(2,1)S(1)}, bf16[16,1792]{1,0:T(8,128)(2,1)S(1)}, u32[]{:S(2)}, u32[]{:S(2)}) %collective-permute-start.6) | collective-permute-done | bytes 57376 | tf_op jit(solution)/shard_map/ppermute | solution.py:53
  22.7 2.4 %collective-permute-start.7 = (bf16[32,1792]{1,0:T(8,128)(2,1)S(1)}, bf16[32,1792]{1,0:T(8,128)(2,1)S(1)}, u32[]{:S(2)}, u32[]{:S(2)}) collective-permute-start(bf16[32,1792]{1,0:T(8,128)(2,1)S(1)} %double.2.refs_0_), channel_id=1, source_target_pairs={{0,16},{1,17},{2,18},{3,19},{4,20},{5,21},{6,22},{7,23},{8,24},{9,... | collective-permute-start | bytes 344072 | tf_op jit(solution)/shard_map/ppermute | solution.py:53
  25.1 0.0 collective-permute-start.8
  25.1 4.6 %collective-permute-done.7.refs_1_ = bf16[32,1792]{1,0:T(8,128)(2,1)S(1)} collective-permute-done((bf16[32,1792]{1,0:T(8,128)(2,1)S(1)}, bf16[32,1792]{1,0:T(8,128)(2,1)S(1)}, u32[]{:S(2)}, u32[]{:S(2)}) %collective-permute-start.7) | collective-permute-done | bytes 114720 | tf_op jit(solution)/shard_map/ppermute | solution.py:53
  29.8 0.1 collective-permute-start.11
  29.9 0.5 collective-permute-start.10
  30.3 0.0 collective-permute-done.3.refs_2_.refs_1_
  30.3 0.1 collective-permute-start.9
  30.4 0.0 collective-permute-done.8.refs_5_.refs_4_
  30.4 0.9 collective-permute-done.11.refs_8_.refs_7_
  31.3 0.4 collective-permute-done.10.refs_7_.refs_6_
  31.7 0.4 collective-permute-done.9.refs_6_.refs_5_
  32.1 0.2 collective-permute-start.16
  32.3 2.6 %collective-permute-start.15 = (bf16[64,1792]{1,0:T(8,128)(2,1)S(1)}, bf16[64,1792]{1,0:T(8,128)(2,1)S(1)}, u32[]{:S(2)}, u32[]{:S(2)}) collective-permute-start(bf16[64,1792]{1,0:T(8,128)(2,1)S(1)} %stack_cotangents.1.refs_10_.refs_0_), channel_id=1, source_target_pairs={{0,6},{1,7},{2,4},{3,5},{4,2},{5,3},{6,0},{7,1},{8,14},{9,15},{10,... | collective-permute-start | bytes 688136 | tf_op jit(solution)/shard_map/ppermute | solution.py:53
  34.9 0.5 collective-permute-start.14
  35.4 0.4 collective-permute-start.13
  35.8 13.5 %gate_up.1 = (bf16[4,64,1792]{2,1,0:T(8,128)(2,1)S(1)}, bf16[64,128]{1,0:T(8,128)(2,1)S(1)}, bf16[128,64]{1,0:T(8,128)(2,1)S(1)}, f32[64,128]{1,0:T(8,128)S(1)},...) custom-call(bf16[64,1920]{1,0:T(8,128)(2,1)S(1)} %get-tuple-element.42.refs_1_.refs_0_, ...), custom_call_target="tpu_custom_call" | custom-call | flops 46000001024 | tf_op jit(solution)/shard_map/gate_up/pallas_call | solution.py:83
  49.2 0.0 collective-permute-done.15.refs_3_
  49.3 0.1 collective-permute-start.19
  49.3 0.5 collective-permute-start.18
  49.8 0.1 collective-permute-start.17
  49.9 7.2 %forward.1 = (bf16[2,2,64,1792]{3,2,1,0:T(8,128)(2,1)S(1)}, bf16[2,2,64,1792]{3,2,1,0:T(8,128)(2,1)S(1)}) custom-call(bf16[2,32,608]{2,1,0:T(8,128)(2,1)S(1)} %get-tuple-element.44.act_ref.refs_0_, f32[64,128]{1,0:T(8,128)S(1)} %get-tuple-element.45.gate_ref.refs_9_, bf16[128,64]{1,0:T(8,128)(2,1)S(1)} %get-tuple-element.46.back_ref, ...), custom_call_target="tpu_custom_call" | custom-call | flops 46000001024 | tf_op jit(solution)/shard_map/forward/pallas_call | solution.py:83
  57.1 0.5 collective-permute-start.12
  57.7 8.5 %hidden_grads.1 = (bf16[4,64,1792]{2,1,0:T(8,128)(2,1)S(1)}, bf16[2,32,608]{2,1,0:T(8,128)(2,1)S(1)}, bf16[2,32,608]{2,1,0:T(8,128)(2,1)S(1)}) custom-call(bf16[64,1792]{1,0:T(8,128)(2,1)S(1)} %stack_cotangents.1.refs_10_.refs_0_, bf16[64,1792]{1,0:T(8,128)(2,1)S(1)} %collective-permute-done.13.refs_1_, ...), custom_call_target="tpu_custom_call" | custom-call | flops 46000001024 | tf_op jit(solution)/shard_map/hidden_grads/pallas_call | solution.py:83
  66.2 0.2 mixed_cores.1
  66.4 1.7 %collective-permute-start.20 = (bf16[64,1792]{1,0:T(8,128)(2,1)S(1)}, bf16[64,1792]{1,0:T(8,128)(2,1)S(1)}, u32[]{:S(2)}, u32[]{:S(2)}) collective-permute-start(bf16[64,1792]{1,0:T(8,128)(2,1)S(1)} %get-tuple-element.54), channel_id=1, source_target_pairs={{0,2},{1,3},{2,0},{3,1},{4,6},{5,7},{6,4},{7,5},{8,10},{9,11},{10,... | collective-permute-start | bytes 688136 | tf_op jit(solution)/shard_map/ppermute | solution.py:53
  68.2 1.5 %collective-permute-start.21 = (bf16[64,1792]{1,0:T(8,128)(2,1)S(1)}, bf16[64,1792]{1,0:T(8,128)(2,1)S(1)}, u32[]{:S(2)}, u32[]{:S(2)}) collective-permute-start(bf16[64,1792]{1,0:T(8,128)(2,1)S(1)} %get-tuple-element.55), channel_id=1, source_target_pairs={{0,4},{1,5},{2,6},{3,7},{4,0},{5,1},{6,2},{7,3},{8,12},{9,13},{10,... | collective-permute-start | bytes 688136 | tf_op jit(solution)/shard_map/ppermute | solution.py:53
  69.7 0.3 collective-permute-start.22
  70.0 9.1 %backward.1 = (bf16[2,2,64,1792]{3,2,1,0:T(8,128)(2,1)S(1)}, bf16[2,2,64,1792]{3,2,1,0:T(8,128)(2,1)S(1)}) custom-call(bf16[2,32,608]{2,1,0:T(8,128)(2,1)S(1)} %get-tuple-element.52.refs_2_.dg_ref.refs_0_, bf16[2,32,608]{2,1,0:T(8,128)(2,1)S(1)} %get-tuple-element.57.du_ref.refs_1_, bf16[128,64]{1,0:T(8,128)(2,1)S(1)} %get-tuple-element.46.back_ref, ...), custom_call_target="tpu_custom_call" | custom-call | flops 46000001024 | tf_op jit(solution)/shard_map/backward/pallas_call | solution.py:83
  79.1 0.1 collective-permute-start.26
  79.2 1.0 collective-permute-done.22.refs_3_
  80.2 0.1 mixed_plane.1
  80.3 0.4 collective-permute-start.23
  80.7 3.4 %collective-permute-start.24 = (bf16[16,1792]{1,0:T(8,128)(2,1)S(1)}, bf16[16,1792]{1,0:T(8,128)(2,1)S(1)}, u32[]{:S(2)}, u32[]{:S(2)}) collective-permute-start(bf16[16,1792]{1,0:T(8,128)(2,1)S(1)} %get-tuple-element.61), channel_id=1, source_target_pairs={{0,16},{1,17},{2,18},{3,19},{4,20},{5,21},{6,22},{7,23},{8,24},{9,... | collective-permute-start | bytes 172040 | tf_op jit(solution)/shard_map/ppermute | solution.py:53
  84.1 9.2 %grad_down.1 = (bf16[2,608,7168]{2,1,0:T(8,128)(2,1)}, f32[8,128]{1,0:T(8,128)S(1)}) custom-call(bf16[2,32,608]{2,1,0:T(8,128)(2,1)S(1)} %get-tuple-element.44.act_ref.refs_0_, bf16[4,64,1792]{2,1,0:T(8,128)(2,1)S(1)} %get-tuple-element.63.refs_1_, bf16[16,1792]{1,0:T(8,128)(2,1)S(1)} %get-tuple-element.59.refs_2_.refs_0_), custom_call_target="tpu_custom_call" | custom-call | flops 46000001024 | tf_op jit(solution)/shard_map/grad_down/pallas_call | solution.py:83
  93.3 0.2 tokens_cores.1
  93.5 1.6 %collective-permute-start.27 = (bf16[64,1792]{1,0:T(8,128)(2,1)S(1)}, bf16[64,1792]{1,0:T(8,128)(2,1)S(1)}, u32[]{:S(2)}, u32[]{:S(2)}) collective-permute-start(bf16[64,1792]{1,0:T(8,128)(2,1)S(1)} %get-tuple-element.67), channel_id=1, source_target_pairs={{0,2},{1,3},{2,0},{3,1},{4,6},{5,7},{6,4},{7,5},{8,10},{9,11},{10,... | collective-permute-start | bytes 688136 | tf_op jit(solution)/shard_map/ppermute | solution.py:53
  95.1 1.5 %collective-permute-start.28 = (bf16[64,1792]{1,0:T(8,128)(2,1)S(1)}, bf16[64,1792]{1,0:T(8,128)(2,1)S(1)}, u32[]{:S(2)}, u32[]{:S(2)}) collective-permute-start(bf16[64,1792]{1,0:T(8,128)(2,1)S(1)} %get-tuple-element.68), channel_id=1, source_target_pairs={{0,4},{1,5},{2,6},{3,7},{4,0},{5,1},{6,2},{7,3},{8,12},{9,13},{10,... | collective-permute-start | bytes 688136 | tf_op jit(solution)/shard_map/ppermute | solution.py:53
  96.6 0.5 collective-permute-start.29
  97.1 13.4 %grad_gate_up.1 = (bf16[2,608,7168]{2,1,0:T(8,128)(2,1)}, bf16[2,608,7168]{2,1,0:T(8,128)(2,1)}, f32[8,128]{1,0:T(8,128)S(1)}) custom-call(bf16[2,32,608]{2,1,0:T(8,128)(2,1)S(1)} %get-tuple-element.52.refs_2_.dg_ref.refs_0_, bf16[2,32,608]{2,1,0:T(8,128)(2,1)S(1)} %get-tuple-element.57.du_ref.refs_1_, bf16[4,64,1792]{2,1,0:T(8,128)(2,1)S(1)} %get-tuple-element.70.refs_2_, ...), custom_call_target="tpu_custom_call" | custom-call | flops 46000001024 | tf_op jit(solution)/shard_map/grad_gate_up/pallas_call | solution.py:83
  110.5 0.6 collective-permute-start.25
  111.1 0.1 tokens_plane.1
  111.2 0.1 collective-permute-start.30
  111.3 3.8 %collective-permute-start.31 = (bf16[16,1792]{1,0:T(8,128)(2,1)S(1)}, bf16[16,1792]{1,0:T(8,128)(2,1)S(1)}, u32[]{:S(2)}, u32[]{:S(2)}) collective-permute-start(bf16[16,1792]{1,0:T(8,128)(2,1)S(1)} %get-tuple-element.74), channel_id=1, source_target_pairs={{0,16},{1,17},{2,18},{3,19},{4,20},{5,21},{6,22},{7,23},{8,24},{9,... | collective-permute-start | bytes 172040 | tf_op jit(solution)/shard_map/ppermute | solution.py:53
  115.1 0.6 collective-permute-start.32
  115.7 0.9 collective-permute-done.25.refs_3_
  116.6 0.7 mixed_z.1
  117.2 1.2 %collective-permute-done.31.refs_2_ = bf16[16,1792]{1,0:T(8,128)(2,1)S(1)} collective-permute-done((bf16[16,1792]{1,0:T(8,128)(2,1)S(1)}, bf16[16,1792]{1,0:T(8,128)(2,1)S(1)}, u32[]{:S(2)}, u32[]{:S(2)}) %collective-permute-start.31) | collective-permute-done | bytes 57376 | tf_op jit(solution)/shard_map/ppermute | solution.py:53
  118.4 2.6 %collective-permute-done.32.refs_3_ = bf16[16,1792]{1,0:T(8,128)(2,1)S(1)} collective-permute-done((bf16[16,1792]{1,0:T(8,128)(2,1)S(1)}, bf16[16,1792]{1,0:T(8,128)(2,1)S(1)}, u32[]{:S(2)}, u32[]{:S(2)}) %collective-permute-start.32) | collective-permute-done | bytes 57376 | tf_op jit(solution)/shard_map/ppermute | solution.py:53
  121.0 0.7 tokens_z.1
  (27 shorter events, 0.1 us)
Async XLA Ops:
  2.1 0.8 copy-start
  3.0 11.9 %copy-start.1 = (bf16[16,1792]{1,0:T(8,128)(2,1)S(1)}, bf16[16,1792]{1,0:T(8,128)(2,1)}, u32[]{:S(2)}) copy-start(bf16[16,1792]{1,0:T(8,128)(2,1)} %refs_4_.1) | copy-start | bytes 172036
  3.1 11.8 %collective-permute-start.2 = (bf16[16,1920]{1,0:T(8,128)(2,1)S(1)}, bf16[16,1920]{1,0:T(8,128)(2,1)S(1)}, u32[]{:S(2)}, u32[]{:S(2)}) collective-permute-start(bf16[16,1920]{1,0:T(8,128)(2,1)S(1)} %pack.1._.refs_0_), channel_id=1, source_target_pairs={{0,24},{1,25},{2,26},{3,27},{4,28},{5,29},{6,30},{7,31},{8,16},{9,... | collective-permute-start | bytes 184328 | tf_op jit(solution)/shard_map/ppermute | solution.py:53
  8.2 6.7 %collective-permute-start.1 = (bf16[16,1920]{1,0:T(8,128)(2,1)S(1)}, bf16[16,1920]{1,0:T(8,128)(2,1)S(1)}, u32[]{:S(2)}, u32[]{:S(2)}) collective-permute-start(bf16[16,1920]{1,0:T(8,128)(2,1)S(1)} %pack.1._.refs_0_), channel_id=1, source_target_pairs={{0,16},{1,17},{2,18},{3,19},{4,20},{5,21},{6,22},{7,23},{8,24},{9,... | collective-permute-start | bytes 184328 | tf_op jit(solution)/shard_map/ppermute | solution.py:53
  8.2 6.7 %collective-permute-start = (bf16[16,1920]{1,0:T(8,128)(2,1)S(1)}, bf16[16,1920]{1,0:T(8,128)(2,1)S(1)}, u32[]{:S(2)}, u32[]{:S(2)}) collective-permute-start(bf16[16,1920]{1,0:T(8,128)(2,1)S(1)} %pack.1._.refs_0_), channel_id=1, source_target_pairs={{0,8},{1,9},{2,10},{3,11},{4,12},{5,13},{6,14},{7,15},{8,0},{9,1},... | collective-permute-start | bytes 184328 | tf_op jit(solution)/shard_map/ppermute | solution.py:53
  15.0 14.8 %collective-permute-start.5 = (bf16[64,1920]{1,0:T(8,128)(2,1)S(1)}, bf16[64,1920]{1,0:T(8,128)(2,1)S(1)}, u32[]{:S(2)}, u32[]{:S(2)}) collective-permute-start(bf16[64,1920]{1,0:T(8,128)(2,1)S(1)} %get-tuple-element.42.refs_1_.refs_0_), channel_id=1, source_target_pairs={{0,6},{1,7},{2,4},{3,5},{4,2},{5,3},{6,0},{7,1},{8,14},{9,15},{10,... | collective-permute-start | bytes 737288 | tf_op jit(solution)/shard_map/ppermute | solution.py:53
  17.6 12.2 %collective-permute-start.4 = (bf16[64,1920]{1,0:T(8,128)(2,1)S(1)}, bf16[64,1920]{1,0:T(8,128)(2,1)S(1)}, u32[]{:S(2)}, u32[]{:S(2)}) collective-permute-start(bf16[64,1920]{1,0:T(8,128)(2,1)S(1)} %get-tuple-element.42.refs_1_.refs_0_), channel_id=1, source_target_pairs={{0,2},{1,3},{2,0},{3,1},{4,6},{5,7},{6,4},{7,5},{8,10},{9,11},{10,... | collective-permute-start | bytes 737288 | tf_op jit(solution)/shard_map/ppermute | solution.py:53
  18.1 12.2 %collective-permute-start.3 = (bf16[64,1920]{1,0:T(8,128)(2,1)S(1)}, bf16[64,1920]{1,0:T(8,128)(2,1)S(1)}, u32[]{:S(2)}, u32[]{:S(2)}) collective-permute-start(bf16[64,1920]{1,0:T(8,128)(2,1)S(1)} %get-tuple-element.42.refs_1_.refs_0_), channel_id=1, source_target_pairs={{0,4},{1,5},{2,6},{3,7},{4,0},{5,1},{6,2},{7,3},{8,12},{9,13},{10,... | collective-permute-start | bytes 737288 | tf_op jit(solution)/shard_map/ppermute | solution.py:53
  18.5 4.2 %collective-permute-start.6 = (bf16[16,1792]{1,0:T(8,128)(2,1)S(1)}, bf16[16,1792]{1,0:T(8,128)(2,1)S(1)}, u32[]{:S(2)}, u32[]{:S(2)}) collective-permute-start(bf16[16,1792]{1,0:T(8,128)(2,1)S(1)} %get-tuple-element.43.refs_0_), channel_id=1, source_target_pairs={{0,8},{1,9},{2,10},{3,11},{4,12},{5,13},{6,14},{7,15},{8,0},{9,1},... | collective-permute-start | bytes 172040 | tf_op jit(solution)/shard_map/ppermute | solution.py:53
  22.7 7.0 %collective-permute-start.7 = (bf16[32,1792]{1,0:T(8,128)(2,1)S(1)}, bf16[32,1792]{1,0:T(8,128)(2,1)S(1)}, u32[]{:S(2)}, u32[]{:S(2)}) collective-permute-start(bf16[32,1792]{1,0:T(8,128)(2,1)S(1)} %double.2.refs_0_), channel_id=1, source_target_pairs={{0,16},{1,17},{2,18},{3,19},{4,20},{5,21},{6,22},{7,23},{8,24},{9,... | collective-permute-start | bytes 344072 | tf_op jit(solution)/shard_map/ppermute | solution.py:53
  25.1 5.4 %collective-permute-start.8 = (bf16[64,1920]{1,0:T(8,128)(2,1)S(1)}, bf16[64,1920]{1,0:T(8,128)(2,1)S(1)}, u32[]{:S(2)}, u32[]{:S(2)}) collective-permute-start(bf16[64,1920]{1,0:T(8,128)(2,1)S(1)} %get-tuple-element.42.refs_1_.refs_0_), channel_id=1, source_target_pairs={{0,1},{1,0},{2,3},{3,2},{4,5},{5,4},{6,7},{7,6},{8,9},{9,8},{10,11... | collective-permute-start | bytes 737288 | tf_op jit(solution)/shard_map/ppermute | solution.py:53
  29.8 1.6 %collective-permute-start.11 = (bf16[64,1920]{1,0:T(8,128)(2,1)S(1)}, bf16[64,1920]{1,0:T(8,128)(2,1)S(1)}, u32[]{:S(2)}, u32[]{:S(2)}) collective-permute-start(bf16[64,1920]{1,0:T(8,128)(2,1)S(1)} %relay.1.refs_4_.refs_3_), channel_id=1, source_target_pairs={{0,1},{1,0},{2,3},{3,2},{4,5},{5,4},{6,7},{7,6},{8,9},{9,8},{10,11... | collective-permute-start | bytes 737288 | tf_op jit(solution)/shard_map/ppermute | solution.py:53
  29.9 1.8 %collective-permute-start.10 = (bf16[64,1920]{1,0:T(8,128)(2,1)S(1)}, bf16[64,1920]{1,0:T(8,128)(2,1)S(1)}, u32[]{:S(2)}, u32[]{:S(2)}) collective-permute-start(bf16[64,1920]{1,0:T(8,128)(2,1)S(1)} %collective-permute-done.4.refs_3_.refs_2_), channel_id=1, source_target_pairs={{0,1},{1,0},{2,3},{3,2},{4,5},{5,4},{6,7},{7,6},{8,9},{9,8},{10,11... | collective-permute-start | bytes 737288 | tf_op jit(solution)/shard_map/ppermute | solution.py:53
  30.3 1.7 %collective-permute-start.9 = (bf16[64,1920]{1,0:T(8,128)(2,1)S(1)}, bf16[64,1920]{1,0:T(8,128)(2,1)S(1)}, u32[]{:S(2)}, u32[]{:S(2)}) collective-permute-start(bf16[64,1920]{1,0:T(8,128)(2,1)S(1)} %collective-permute-done.3.refs_2_.refs_1_), channel_id=1, source_target_pairs={{0,1},{1,0},{2,3},{3,2},{4,5},{5,4},{6,7},{7,6},{8,9},{9,8},{10,11... | collective-permute-start | bytes 737288 | tf_op jit(solution)/shard_map/ppermute | solution.py:53
  32.1 25.6 %collective-permute-start.16 = (bf16[64,1792]{1,0:T(8,128)(2,1)S(1)}, bf16[64,1792]{1,0:T(8,128)(2,1)S(1)}, u32[]{:S(2)}, u32[]{:S(2)}) collective-permute-start(bf16[64,1792]{1,0:T(8,128)(2,1)S(1)} %stack_cotangents.1.refs_10_.refs_0_), channel_id=1, source_target_pairs={{0,1},{1,0},{2,3},{3,2},{4,5},{5,4},{6,7},{7,6},{8,9},{9,8},{10,11... | collective-permute-start | bytes 688136 | tf_op jit(solution)/shard_map/ppermute | solution.py:53
  32.3 17.0 %collective-permute-start.15 = (bf16[64,1792]{1,0:T(8,128)(2,1)S(1)}, bf16[64,1792]{1,0:T(8,128)(2,1)S(1)}, u32[]{:S(2)}, u32[]{:S(2)}) collective-permute-start(bf16[64,1792]{1,0:T(8,128)(2,1)S(1)} %stack_cotangents.1.refs_10_.refs_0_), channel_id=1, source_target_pairs={{0,6},{1,7},{2,4},{3,5},{4,2},{5,3},{6,0},{7,1},{8,14},{9,15},{10,... | collective-permute-start | bytes 688136 | tf_op jit(solution)/shard_map/ppermute | solution.py:53
  34.9 14.5 %collective-permute-start.14 = (bf16[64,1792]{1,0:T(8,128)(2,1)S(1)}, bf16[64,1792]{1,0:T(8,128)(2,1)S(1)}, u32[]{:S(2)}, u32[]{:S(2)}) collective-permute-start(bf16[64,1792]{1,0:T(8,128)(2,1)S(1)} %stack_cotangents.1.refs_10_.refs_0_), channel_id=1, source_target_pairs={{0,2},{1,3},{2,0},{3,1},{4,6},{5,7},{6,4},{7,5},{8,10},{9,11},{10,... | collective-permute-start | bytes 688136 | tf_op jit(solution)/shard_map/ppermute | solution.py:53
  35.4 14.4 %collective-permute-start.13 = (bf16[64,1792]{1,0:T(8,128)(2,1)S(1)}, bf16[64,1792]{1,0:T(8,128)(2,1)S(1)}, u32[]{:S(2)}, u32[]{:S(2)}) collective-permute-start(bf16[64,1792]{1,0:T(8,128)(2,1)S(1)} %stack_cotangents.1.refs_10_.refs_0_), channel_id=1, source_target_pairs={{0,4},{1,5},{2,6},{3,7},{4,0},{5,1},{6,2},{7,3},{8,12},{9,13},{10,... | collective-permute-start | bytes 688136 | tf_op jit(solution)/shard_map/ppermute | solution.py:53
  49.3 8.4 %collective-permute-start.19 = (bf16[64,1792]{1,0:T(8,128)(2,1)S(1)}, bf16[64,1792]{1,0:T(8,128)(2,1)S(1)}, u32[]{:S(2)}, u32[]{:S(2)}) collective-permute-start(bf16[64,1792]{1,0:T(8,128)(2,1)S(1)} %collective-permute-done.15.refs_3_), channel_id=1, source_target_pairs={{0,1},{1,0},{2,3},{3,2},{4,5},{5,4},{6,7},{7,6},{8,9},{9,8},{10,11... | collective-permute-start | bytes 688136 | tf_op jit(solution)/shard_map/ppermute | solution.py:53
  49.3 8.3 %collective-permute-start.18 = (bf16[64,1792]{1,0:T(8,128)(2,1)S(1)}, bf16[64,1792]{1,0:T(8,128)(2,1)S(1)}, u32[]{:S(2)}, u32[]{:S(2)}) collective-permute-start(bf16[64,1792]{1,0:T(8,128)(2,1)S(1)} %collective-permute-done.14.refs_2_), channel_id=1, source_target_pairs={{0,1},{1,0},{2,3},{3,2},{4,5},{5,4},{6,7},{7,6},{8,9},{9,8},{10,11... | collective-permute-start | bytes 688136 | tf_op jit(solution)/shard_map/ppermute | solution.py:53
  49.8 7.8 %collective-permute-start.17 = (bf16[64,1792]{1,0:T(8,128)(2,1)S(1)}, bf16[64,1792]{1,0:T(8,128)(2,1)S(1)}, u32[]{:S(2)}, u32[]{:S(2)}) collective-permute-start(bf16[64,1792]{1,0:T(8,128)(2,1)S(1)} %collective-permute-done.13.refs_1_), channel_id=1, source_target_pairs={{0,1},{1,0},{2,3},{3,2},{4,5},{5,4},{6,7},{7,6},{8,9},{9,8},{10,11... | collective-permute-start | bytes 688136 | tf_op jit(solution)/shard_map/ppermute | solution.py:53
  57.1 9.1 %collective-permute-start.12 = (bf16[2,2,64,1792]{3,2,1,0:T(8,128)(2,1)S(1)}, bf16[2,2,64,1792]{3,2,1,0:T(8,128)(2,1)S(1)}, u32[]{:S(2)}, u32[]{:S(2)}) collective-permute-start(bf16[2,2,64,1792]{3,2,1,0:T(8,128)(2,1)S(1)} %get-tuple-element.48), channel_id=1, source_target_pairs={{0,1},{1,0},{2,3},{3,2},{4,5},{5,4},{6,7},{7,6},{8,9},{9,8},{10,11... | collective-permute-start | bytes 2752520 | tf_op jit(solution)/shard_map/ppermute | solution.py:53
  66.4 12.7 %collective-permute-start.20 = (bf16[64,1792]{1,0:T(8,128)(2,1)S(1)}, bf16[64,1792]{1,0:T(8,128)(2,1)S(1)}, u32[]{:S(2)}, u32[]{:S(2)}) collective-permute-start(bf16[64,1792]{1,0:T(8,128)(2,1)S(1)} %get-tuple-element.54), channel_id=1, source_target_pairs={{0,2},{1,3},{2,0},{3,1},{4,6},{5,7},{6,4},{7,5},{8,10},{9,11},{10,... | collective-permute-start | bytes 688136 | tf_op jit(solution)/shard_map/ppermute | solution.py:53
  68.2 11.0 %collective-permute-start.21 = (bf16[64,1792]{1,0:T(8,128)(2,1)S(1)}, bf16[64,1792]{1,0:T(8,128)(2,1)S(1)}, u32[]{:S(2)}, u32[]{:S(2)}) collective-permute-start(bf16[64,1792]{1,0:T(8,128)(2,1)S(1)} %get-tuple-element.55), channel_id=1, source_target_pairs={{0,4},{1,5},{2,6},{3,7},{4,0},{5,1},{6,2},{7,3},{8,12},{9,13},{10,... | collective-permute-start | bytes 688136 | tf_op jit(solution)/shard_map/ppermute | solution.py:53
  69.7 10.5 %collective-permute-start.22 = (bf16[64,1792]{1,0:T(8,128)(2,1)S(1)}, bf16[64,1792]{1,0:T(8,128)(2,1)S(1)}, u32[]{:S(2)}, u32[]{:S(2)}) collective-permute-start(bf16[64,1792]{1,0:T(8,128)(2,1)S(1)} %get-tuple-element.56), channel_id=1, source_target_pairs={{0,6},{1,7},{2,4},{3,5},{4,2},{5,3},{6,0},{7,1},{8,14},{9,15},{10,... | collective-permute-start | bytes 688136 | tf_op jit(solution)/shard_map/ppermute | solution.py:53
  79.1 14.2 %collective-permute-start.26 = (bf16[2,2,64,1792]{3,2,1,0:T(8,128)(2,1)S(1)}, bf16[2,2,64,1792]{3,2,1,0:T(8,128)(2,1)S(1)}, u32[]{:S(2)}, u32[]{:S(2)}) collective-permute-start(bf16[2,2,64,1792]{3,2,1,0:T(8,128)(2,1)S(1)} %get-tuple-element.65), channel_id=1, source_target_pairs={{0,1},{1,0},{2,3},{3,2},{4,5},{5,4},{6,7},{7,6},{8,9},{9,8},{10,11... | collective-permute-start | bytes 2752520 | tf_op jit(solution)/shard_map/ppermute | solution.py:53
  80.3 34.8 %collective-permute-start.23 = (bf16[16,1792]{1,0:T(8,128)(2,1)S(1)}, bf16[16,1792]{1,0:T(8,128)(2,1)S(1)}, u32[]{:S(2)}, u32[]{:S(2)}) collective-permute-start(bf16[16,1792]{1,0:T(8,128)(2,1)S(1)} %get-tuple-element.60), channel_id=1, source_target_pairs={{0,8},{1,9},{2,10},{3,11},{4,12},{5,13},{6,14},{7,15},{8,0},{9,1},... | collective-permute-start | bytes 172040 | tf_op jit(solution)/shard_map/ppermute | solution.py:53
  80.7 34.9 %collective-permute-start.24 = (bf16[16,1792]{1,0:T(8,128)(2,1)S(1)}, bf16[16,1792]{1,0:T(8,128)(2,1)S(1)}, u32[]{:S(2)}, u32[]{:S(2)}) collective-permute-start(bf16[16,1792]{1,0:T(8,128)(2,1)S(1)} %get-tuple-element.61), channel_id=1, source_target_pairs={{0,16},{1,17},{2,18},{3,19},{4,20},{5,21},{6,22},{7,23},{8,24},{9,... | collective-permute-start | bytes 172040 | tf_op jit(solution)/shard_map/ppermute | solution.py:53
  93.5 16.9 %collective-permute-start.27 = (bf16[64,1792]{1,0:T(8,128)(2,1)S(1)}, bf16[64,1792]{1,0:T(8,128)(2,1)S(1)}, u32[]{:S(2)}, u32[]{:S(2)}) collective-permute-start(bf16[64,1792]{1,0:T(8,128)(2,1)S(1)} %get-tuple-element.67), channel_id=1, source_target_pairs={{0,2},{1,3},{2,0},{3,1},{4,6},{5,7},{6,4},{7,5},{8,10},{9,11},{10,... | collective-permute-start | bytes 688136 | tf_op jit(solution)/shard_map/ppermute | solution.py:53
  95.1 16.0 %collective-permute-start.28 = (bf16[64,1792]{1,0:T(8,128)(2,1)S(1)}, bf16[64,1792]{1,0:T(8,128)(2,1)S(1)}, u32[]{:S(2)}, u32[]{:S(2)}) collective-permute-start(bf16[64,1792]{1,0:T(8,128)(2,1)S(1)} %get-tuple-element.68), channel_id=1, source_target_pairs={{0,4},{1,5},{2,6},{3,7},{4,0},{5,1},{6,2},{7,3},{8,12},{9,13},{10,... | collective-permute-start | bytes 688136 | tf_op jit(solution)/shard_map/ppermute | solution.py:53
  96.6 14.5 %collective-permute-start.29 = (bf16[64,1792]{1,0:T(8,128)(2,1)S(1)}, bf16[64,1792]{1,0:T(8,128)(2,1)S(1)}, u32[]{:S(2)}, u32[]{:S(2)}) collective-permute-start(bf16[64,1792]{1,0:T(8,128)(2,1)S(1)} %get-tuple-element.69), channel_id=1, source_target_pairs={{0,6},{1,7},{2,4},{3,5},{4,2},{5,3},{6,0},{7,1},{8,14},{9,15},{10,... | collective-permute-start | bytes 688136 | tf_op jit(solution)/shard_map/ppermute | solution.py:53
  110.5 6.1 %collective-permute-start.25 = (bf16[16,1792]{1,0:T(8,128)(2,1)S(1)}, bf16[16,1792]{1,0:T(8,128)(2,1)S(1)}, u32[]{:S(2)}, u32[]{:S(2)}) collective-permute-start(bf16[16,1792]{1,0:T(8,128)(2,1)S(1)} %get-tuple-element.62), channel_id=1, source_target_pairs={{0,24},{1,25},{2,26},{3,27},{4,28},{5,29},{6,30},{7,31},{8,16},{9,... | collective-permute-start | bytes 172040 | tf_op jit(solution)/shard_map/ppermute | solution.py:53
  111.2 6.0 %collective-permute-start.30 = (bf16[16,1792]{1,0:T(8,128)(2,1)S(1)}, bf16[16,1792]{1,0:T(8,128)(2,1)S(1)}, u32[]{:S(2)}, u32[]{:S(2)}) collective-permute-start(bf16[16,1792]{1,0:T(8,128)(2,1)S(1)} %get-tuple-element.73), channel_id=1, source_target_pairs={{0,8},{1,9},{2,10},{3,11},{4,12},{5,13},{6,14},{7,15},{8,0},{9,1},... | collective-permute-start | bytes 172040 | tf_op jit(solution)/shard_map/ppermute | solution.py:53
  111.3 7.1 %collective-permute-start.31 = (bf16[16,1792]{1,0:T(8,128)(2,1)S(1)}, bf16[16,1792]{1,0:T(8,128)(2,1)S(1)}, u32[]{:S(2)}, u32[]{:S(2)}) collective-permute-start(bf16[16,1792]{1,0:T(8,128)(2,1)S(1)} %get-tuple-element.74), channel_id=1, source_target_pairs={{0,16},{1,17},{2,18},{3,19},{4,20},{5,21},{6,22},{7,23},{8,24},{9,... | collective-permute-start | bytes 172040 | tf_op jit(solution)/shard_map/ppermute | solution.py:53
  115.1 6.0 %collective-permute-start.32 = (bf16[16,1792]{1,0:T(8,128)(2,1)S(1)}, bf16[16,1792]{1,0:T(8,128)(2,1)S(1)}, u32[]{:S(2)}, u32[]{:S(2)}) collective-permute-start(bf16[16,1792]{1,0:T(8,128)(2,1)S(1)} %get-tuple-element.75), channel_id=1, source_target_pairs={{0,24},{1,25},{2,26},{3,27},{4,28},{5,29},{6,30},{7,31},{8,16},{9,... | collective-permute-start | bytes 172040 | tf_op jit(solution)/shard_map/ppermute | solution.py:53

commit v3 on v2

--- a/solution.py
+++ b/solution.py
@@ -56,11 +56,11 @@
         return [mine] + [self.shift(mine, dz=k) for k in range(1, self.nz)]
 
     def doubled_along_z(self, mine):
-        column, k = mine, 1
+        columns, k = [mine], 1
         while k < self.nz:
-            column = stack([column, self.shift(column, dz=k)], [], "double")
+            columns.append(stack([columns[-1], self.shift(columns[-1], dz=k)], [], "double"))
             k *= 2
-        return column
+        return columns
 
     def over_plane(self, column):
         return {(a, b): self.shift(column, dx=a, dy=b) if a or b else column for a, b in self.square}
@@ -101,34 +101,6 @@
 ANYWHERE = pl.BlockSpec(memory_space=pl.ANY)
 
 
-def hold_kernel(source, _, held, sems):
-    local, pieces = sems.shape
-    part = source.shape[1] // pieces
-    copies = []
-    for e in range(local):
-        for k in range(pieces):
-            at = (e, pl.ds(k * part, part))
-            copies.append(pltpu.make_async_copy(source.at[at], held.at[at], sems.at[e, k]))
-    for copy in copies:
-        copy.start()
-    for copy in copies:
-        copy.wait()
-
-
-def hold(weight, after, name):
-    pieces = 2 if weight.shape[1] % 32 == 0 else 1
-    (held,) = call(
-        hold_kernel,
-        name,
-        [pltpu.VMEM(weight.shape, BF16)],
-        [hbm(weight), after],
-        specs=[ANYWHERE] * 2,
-        scratch=[pltpu.SemaphoreType.DMA((weight.shape[0], pieces))],
-        cost=12000,
-    )
-    return held
-
-
 def hbm(weight):
     return pltpu.with_memory_space_constraint(weight, pltpu.HBM)
 
@@ -140,12 +112,9 @@
     high = gates.astype(BF16).astype(F32)
     middle = (gates - high).astype(BF16).astype(F32)
     low = gates - high - middle
-    lane = lax.broadcasted_iota(jnp.int32, (rows, LANES), 1)
-    aux = jnp.zeros((rows, LANES), F32)
-    for k, part in enumerate([ids_ref[...].astype(F32), high, middle, low]):
-        for n in range(2):
-            aux = jnp.where(lane == 2 * k + n, part[:, n : n + 1], aux)
-    out_ref[:, width:] = aux.astype(BF16)
+    fields = jnp.concatenate([ids_ref[...].astype(F32), high, middle, low], axis=0)
+    fields = jnp.pad(fields, ((0, LANES - fields.shape[0]), (0, LANES - rows)))
+    out_ref[:, width:] = jnp.transpose(fields)[:rows].astype(BF16)
 
 
 def stack_kernel(count, later, *refs):
@@ -230,11 +199,13 @@
     return select, gate
 
 
-def streamed(weight, held, sems, starts):
-    depth, width = held.shape[0], held.shape[-1]
+def streamed(weight, held, sems, columns):
+    depth = held.shape[0]
     copies = [
-        pltpu.make_async_copy(weight.at[:, :, pl.ds(start, width)], held.at[k % depth], sems.at[k % depth])
-        for k, start in enumerate(starts)
+        pltpu.make_async_copy(
+            weight.at[:, :, pl.ds(start, size)], held.at[k % depth, :, :, pl.ds(0, size)], sems.at[k % depth]
+        )
+        for k, (start, size) in enumerate(columns)
     ]
     for copy in copies[:depth]:
         copy.start()
@@ -242,9 +213,31 @@
     def each():
         for k, copy in enumerate(copies):
             copy.wait()
-            yield k, held.at[k % depth]
+            size = columns[k][1]
+            yield held[k % depth, :, :, :size].reshape(-1, size)
             if k + depth < len(copies):
                 copies[k + depth].start()
+
+    return each()
+
+
+def kept(weight, held, sems, columns):
+    copies = []
+    for k, (start, size) in enumerate(columns):
+        at = (slice(None), slice(None), pl.ds(start, size))
+        copies.append(pltpu.make_async_copy(weight.at[at], held.at[at], sems.at[k]))
+
+    ahead = 4
+    for copy in copies[:ahead]:
+        copy.start()
+
+    def each():
+        for k, copy in enumerate(copies):
+            copy.wait()
+            start, size = columns[k]
+            yield held[:, :, start : start + size].reshape(-1, size)
+            if k + ahead < len(copies):
+                copies[k + ahead].start()
 
     return each()
 
@@ -260,17 +253,17 @@
         self.column = grid.nz * self.block
         self.blocks = grid.nc * grid.ny * grid.nx
         self.slices = grid.nc * grid.ny
-        self.chunk = 896 if self.width % 896 == 0 else self.width
-        self.per = self.width // self.chunk
-
-    def relative_starts(self):
-        return [
-            pl.multiple_of(self.grid.source(k // self.per) * self.width + k % self.per * self.chunk, self.chunk)
-            for k in range(self.slices * self.per)
-        ]
-
-    def at(self, e):
-        return slice(e * self.rows, (e + 1) * self.rows)
+        self.merged = self.local * self.hidden
+        whole = self.width % 256 == 0 and self.width > 1024
+        self.pieces = [(0, 1024), (1024, self.width - 1024)] if whole else [(0, self.width)]
+
+    def walk(self):
+        return [(k, at, size) for k in range(self.slices) for at, size in self.pieces]
+
+    def own_expert(self):
+        expert = lax.broadcasted_iota(jnp.int32, (self.total, self.merged), 0) >> log2(self.rows)
+        unit = lax.broadcasted_iota(jnp.int32, (self.total, self.merged), 1)
+        return (unit >= expert * self.hidden) & (unit < (expert + 1) * self.hidden)
 
 
 def routed(s, blocks, select):
@@ -281,8 +274,12 @@
 
 def gate_up_kernel(s, *refs):
     blocks = refs[: s.blocks]
-    wg_ref, wu_ref, _, x_ref, select_ref, back_ref, gate_ref, act_ref, p_ref, q_ref, held, sems = refs[s.blocks :]
-    chunks = streamed(wu_ref, held, sems, range(0, s.features, s.chunk))
+    (wg_ref, wu_ref, _, x_ref, select_ref, back_ref, gate_ref, act_ref, p_ref, q_ref, held_ref, room, sems, held_sems) = refs[
+        s.blocks :
+    ]
+    walk = s.walk()
+    columns = [(k * s.width + at, size) for k, at, size in walk]
+    gates, ups = kept(wg_ref, held_ref, held_sems, columns), streamed(wu_ref, room, sems, columns)
     aux = jnp.concatenate([ref[:, s.width :] for ref in blocks[: s.grid.nx]], axis=0)
     select, gate = tables(aux, lax.axis_index("hst") * s.local, s.rows, s.local, s.block)
     gate_ref[...] = jnp.broadcast_to(gate, gate_ref.shape)
@@ -290,61 +287,57 @@
     back_ref[...] = jnp.transpose(select).astype(BF16)
     for k, picked in routed(s, blocks, select.astype(BF16)):
         x_ref[s.grid.source(k)] = picked.astype(BF16)
-    g, u = [0.0] * s.local, [0.0] * s.local
-    for k, weight in chunks:
-        at = k % s.per * s.chunk
-        columns = slice(k * s.chunk, (k + 1) * s.chunk)
-        for e in range(s.local):
-            x = x_ref[k // s.per, s.at(e), at : at + s.chunk]
-            g[e] += dot_t(x, wg_ref[e, :, columns])
-            u[e] += dot_t(x, weight[e])
-    for e in range(s.local):
-        sigma = jax.nn.sigmoid(g[e])
-        act_ref[e] = (g[e] * sigma * u[e]).astype(BF16)
-        p_ref[e] = u[e] * sigma * (1.0 + g[e] * (1.0 - sigma))
-        q_ref[e] = g[e] * sigma
+    g = u = 0.0
+    for (k, at, size), wg, wu in zip(walk, gates, ups):
+        x = x_ref[k, :, at : at + size]
+        g += dot_t(x, wg)
+        u += dot_t(x, wu)
+    sigma = jax.nn.sigmoid(g)
+    mine = s.own_expert()
+    act_ref[...] = jnp.where(mine, g * sigma * u, 0.0).astype(BF16)
+    p_ref[...] = jnp.where(mine, u * sigma * (1.0 + g * (1.0 - sigma)), 0.0)
+    q_ref[...] = jnp.where(mine, g * sigma, 0.0)
 
 
 def hidden_grads_kernel(s, *refs):
     blocks = refs[: s.blocks]
-    select_ref, gate_ref, p_ref, q_ref, w_ref, d_ref, dg_ref, du_ref, held, sems = refs[s.blocks :]
-    chunks = streamed(w_ref, held, sems, range(0, s.features, s.chunk))
+    select_ref, gate_ref, p_ref, q_ref, w_ref, d_ref, dg_ref, du_ref, room, sems = refs[s.blocks :]
+    walk = s.walk()
+    weights = streamed(w_ref, room, sems, [(k * s.width + at, size) for k, at, size in walk])
     for k, picked in routed(s, blocks, select_ref[...]):
         d_ref[s.grid.source(k)] = (picked * gate_ref[:, :1]).astype(BF16)
-    da = [0.0] * s.local
-    for k, weight in chunks:
-        at = k % s.per * s.chunk
-        for e in range(s.local):
-            da[e] += dot_t(d_ref[k // s.per, s.at(e), at : at + s.chunk], weight[e])
-    for e in range(s.local):
-        dg_ref[e] = (da[e] * p_ref[e]).astype(BF16)
-        du_ref[e] = (da[e] * q_ref[e]).astype(BF16)
+    da = 0.0
+    for (k, at, size), weight in zip(walk, weights):
+        da += dot_t(d_ref[k, :, at : at + size], weight)
+    dg_ref[...] = (da * p_ref[...]).astype(BF16)
+    du_ref[...] = (da * q_ref[...]).astype(BF16)
 
 
 def to_tokens(s, k, at, found, back_ref, outs):
     each = s.slices // s.grid.nc
-    sums = dot(back_ref[...], jnp.concatenate(found, axis=0)).astype(BF16)
-    width = sums.shape[-1]
-    outs[k // each][:, k % each, :, at : at + width] = sums.reshape(s.grid.nx, s.column, width)
+    sums = dot(back_ref[...], found.astype(BF16)).astype(BF16)
+    size = sums.shape[-1]
+    outs[k // each][:, k % each, :, at : at + size] = sums.reshape(s.grid.nx, s.column, size)
+
+
+def relative(s, walk):
+    return [(pl.multiple_of(s.grid.source(k) * s.width + at, LANES), size) for k, at, size in walk]
 
 
 def forward_kernel(s, act_ref, gate_ref, back_ref, w_ref, *refs):
-    outs, (held, sems) = refs[:-2], refs[-2:]
-    for k, weight in streamed(w_ref, held, sems, s.relative_starts()):
-        found = [(dot(act_ref[e], weight[e]) * gate_ref[s.at(e), :1]).astype(BF16) for e in range(s.local)]
-        to_tokens(s, k // s.per, k % s.per * s.chunk, found, back_ref, outs)
-
-
-def backward_kernel(s, dg_ref, du_ref, back_ref, wg_ref, wu_ref, _, *refs):
-    outs, (held, sems) = refs[:-2], refs[-2:]
-    starts = s.relative_starts()
-    for k, weight in streamed(wu_ref, held, sems, starts):
-        columns = pl.ds(starts[k], s.chunk)
-        found = [
-            (dot(dg_ref[e], wg_ref[e, :, columns]) + dot(du_ref[e], weight[e])).astype(BF16)
-            for e in range(s.local)
-        ]
-        to_tokens(s, k // s.per, k % s.per * s.chunk, found, back_ref, outs)
+    outs, (room, sems) = refs[:-2], refs[-2:]
+    walk = s.walk()
+    for (k, at, _), weight in zip(walk, streamed(w_ref, room, sems, relative(s, walk))):
+        to_tokens(s, k, at, dot(act_ref[...], weight) * gate_ref[:, :1], back_ref, outs)
+
+
+def backward_kernel(s, dg_ref, du_ref, back_ref, held_ref, wu_ref, _, *refs):
+    outs, (room, sems) = refs[:-2], refs[-2:]
+    walk = s.walk()
+    columns = relative(s, walk)
+    for (k, at, size), (start, _), up in zip(walk, columns, streamed(wu_ref, room, sems, columns)):
+        gate = held_ref[:, :, pl.ds(start, size)].reshape(s.merged, size)
+        to_tokens(s, k, at, dot(dg_ref[...], gate) + dot(du_ref[...], up), back_ref, outs)
 
 
 def grads_kernel(s, count, *refs):
@@ -355,30 +348,25 @@
     def _():
         marker[...] = jnp.zeros_like(marker)
         for left, turn in zip(lefts, turned):
-            for e in range(s.local):
-                turn[e] = jnp.transpose(left[e].astype(F32)).astype(BF16)
-
-    right = rows_ref[0]
+            turn[...] = jnp.transpose(left[...].astype(F32)).astype(BF16)
+
     for turn, out in zip(turned, outs):
-        for e in range(s.local):
-            out[e] = dot(turn[e], right[s.at(e)]).astype(BF16)
+        out[...] = dot(turn[...], rows_ref[0]).astype(BF16).reshape(out.shape)
 
 
 def grads(s, name, lefts, right, after):
-    chunk, per = s.chunk, s.per
-    whole = pl.BlockSpec((s.local, s.rows, s.hidden), lambda i: (0, 0, 0))
     return call(
         functools.partial(grads_kernel, s, len(lefts)),
         name,
         [shaped(BF16, s.local, s.hidden, s.features)] * len(lefts) + [shaped(F32, 8, LANES)],
         [*lefts, right, after],
-        specs=[whole] * len(lefts)
-        + [pl.BlockSpec((1, s.total, chunk), lambda i: (i // per, 0, i % per)), ANYWHERE],
-        out_specs=[pl.BlockSpec((s.local, s.hidden, chunk), lambda i: (0, 0, i))] * len(lefts)
+        specs=[pl.BlockSpec((s.total, s.merged), lambda i: (0, 0))] * len(lefts)
+        + [pl.BlockSpec((1, s.total, s.width), lambda i: (i, 0, 0)), ANYWHERE],
+        out_specs=[pl.BlockSpec((s.local, s.hidden, s.width), lambda i: (0, 0, i))] * len(lefts)
         + [pl.BlockSpec((8, LANES), lambda i: (0, 0))],
-        scratch=[pltpu.VMEM((s.local, s.hidden, s.rows), BF16)] * len(lefts),
-        grid=(s.features // chunk,),
-        limit=8 + 6 * len(lefts),
+        scratch=[pltpu.VMEM((s.merged, s.total), BF16)] * len(lefts),
+        grid=(s.slices,),
+        limit=8 + 12 * len(lefts),
         cost=46000,
     )
 
@@ -388,22 +376,23 @@
     s = Sizes(grid, tokens, w_gate)
 
     (message,) = call(
-        pack_kernel, "pack", [shaped(BF16, s.block, s.width + LANES)], [tokens, expert_ids, gate_values]
+        pack_kernel, "pack", [shaped(BF16, s.block, s.width + LANES)], [tokens, expert_ids.T, gate_values.T]
     )
     x_parts = grid.along_z(message)
-    held_gate = hold(w_gate, message, "hold_gate")
-    x_column, cotangent = stack(x_parts, [held_gate], "stack_tokens", [cotangent])
+    x_column, cotangent = stack(x_parts, [], "stack_tokens", [cotangent])
     x_plane = grid.over_plane(x_column)
-    d_column = grid.doubled_along_z(cotangent)
+    d_halves = grid.doubled_along_z(cotangent)
+    d_column = d_halves[-1]
     last = grid.square[-1]
-    x_plane[last] = stack([x_plane[last]], [d_column], "relay")
+    x_plane[last] = stack([x_plane[last]], [d_halves[-2]], "relay")
     x_blocks = grid.over_cores(x_plane)
     d_column = stack([d_column], x_blocks, "stack_cotangents")
-    streams = [pltpu.VMEM((3, s.local, s.hidden, s.chunk), BF16), pltpu.SemaphoreType.DMA((3,))]
-
-    hidden_shape = (s.local, s.rows, s.hidden)
+    room = max(size for _, size in s.pieces)
+    streams = [pltpu.VMEM((3, s.local, s.hidden, room), BF16), pltpu.SemaphoreType.DMA((3,))]
+
+    hidden_shape = (s.total, s.merged)
     rows_shape = shaped(BF16, s.slices, s.total, s.width)
-    x_rows, select, back, gate, act, p, q = call(
+    x_rows, select, back, gate, act, p, q, held_gate = call(
         functools.partial(gate_up_kernel, s),
         "gate_up",
         [
@@ -414,10 +403,11 @@
             shaped(BF16, *hidden_shape),
             shaped(F32, *hidden_shape),
             shaped(F32, *hidden_shape),
+            pltpu.VMEM(w_gate.shape, BF16),
         ],
-        [*x_blocks, held_gate, hbm(w_up), d_column],
-        specs=[VECTORS] * (s.blocks + 1) + [ANYWHERE] * 2,
-        scratch=streams,
+        [*x_blocks, hbm(w_gate), hbm(w_up), d_column],
+        specs=[VECTORS] * s.blocks + [ANYWHERE] * 3,
+        scratch=[*streams, pltpu.SemaphoreType.DMA((len(s.walk()),))],
         limit=16,
         cost=46000,
     )
@@ -454,11 +444,11 @@
         limit=16,
         cost=46000,
     )
-    mixed_total = back_over_plane(grid, mixed_kept, back_parts[:1], "mixed_plane")
-    grad_down, down_done = grads(s, "grad_down", [act], d_rows, mixed_total[0])
-    mixed = back_along_z(grid, mixed_total, [down_done], "mixed_z")
+    grad_down, down_done = grads(s, "grad_down", [act], d_rows, back_parts[0])
     token_kept = back_over_cores(grid, back_parts, [down_done], "tokens_cores")
-    grad_gate, grad_up, gate_up_done = grads(s, "grad_gate_up", [d_gate, d_up], x_rows, token_kept[0])
+    mixed_total = back_over_plane(grid, mixed_kept, token_kept[:1], "mixed_plane")
+    grad_gate, grad_up, gate_up_done = grads(s, "grad_gate_up", [d_gate, d_up], x_rows, mixed_total[0])
+    mixed = back_along_z(grid, mixed_total, [gate_up_done], "mixed_z")
     token_total = back_over_plane(grid, token_kept, [gate_up_done], "tokens_plane")
     grad_tokens = back_along_z(grid, token_total, [], "tokens_z")
     return mixed, grad_tokens, grad_gate, grad_up, grad_down

time: 122 us -> 130 us (1.066)
  waiting for transfers between devices: 14.8 us -> 24.6 us
  starting transfers between devices: 34.6 us -> 32.3 us
    ppermute x33, waiting for transfers between devices: 14.8 us -> 24.6 us  [shift(): return lax.ppermute(value, AXES, pairs)]
    ppermute x33, starting transfers between devices: 34.6 us -> 32.3 us  [shift(): return lax.ppermute(value, AXES, pairs)]
    unnamed x6 -> x8, local copies, waits for them, and re-layouts: 2.34 us -> 2.99 us
    pallas_call x19 -> x18, Pallas kernels: 69.1 us -> 68.6 us  [call(): pl.pallas_call(kernel, name=name, grid=grid, out_shape=outs, in_specs=spe...]
  transfers between devices with their start and end apart: 33 -> 33, of which waited for: 9 -> 10; matrix products, arithmetic and copies ran while one was open for 0% -> 0% of each run, Pallas kernels for 56% -> 52%
where the time goes in v3:
time: 130 us; the launch traced here: 129 us
  Pallas kernels  68.6 us (53%)
  starting transfers between devices  32.3 us (25%)
  waiting for transfers between devices  24.6 us (19%)
  local copies, waits for them, and re-layouts  2.99 us (2%)
    pallas_call x18, Pallas kernels, call(): pl.pallas_call(kernel, name=name, grid=grid, out_shape=outs, in_specs=spe...  68.6 us
    ppermute x33, starting transfers between devices, shift(): return lax.ppermute(value, AXES, pairs)  32.3 us
    ppermute x33, waiting for transfers between devices, shift(): return lax.ppermute(value, AXES, pairs)  24.6 us
    unnamed x8, local copies, waits for them, and re-layouts  2.99 us
  transfers between devices with their start and end apart: 33, of which 10 were waited for; matrix products, arithmetic and copies ran while one was open for 0% of the time, Pallas kernels for 52%

profile of v3, /device:TPU:0, one launch (start us, length us, event | category | flops | bytes accessed | tf_op | source)
XLA Modules:
  0.0 129.3 jit_solution(2990803035415638269)
XLA Ops:
  0.6 0.8 copy-done.1
  1.5 0.7 copy-done.2
  2.1 0.7 copy-done.3
  2.8 0.1 pack.1.refs_0_
  2.9 5.0 %collective-permute-start.2 = (bf16[16,1920]{1,0:T(8,128)(2,1)S(1)}, bf16[16,1920]{1,0:T(8,128)(2,1)S(1)}, u32[]{:S(2)}, u32[]{:S(2)}) collective-permute-start(bf16[16,1920]{1,0:T(8,128)(2,1)S(1)} %pack.1.refs_0_), channel_id=1, source_target_pairs={{0,24},{1,25},{2,26},{3,27},{4,28},{5,29},{6,30},{7,31},{8,16},{9,... | collective-permute-start | bytes 184328 | tf_op jit(solution)/shard_map/ppermute | solution.py:53
  7.9 0.0 collective-permute-start.1
  7.9 0.6 collective-permute-start
  8.6 1.8 %collective-permute-done.2.refs_3_ = bf16[16,1920]{1,0:T(8,128)(2,1)S(1)} collective-permute-done((bf16[16,1920]{1,0:T(8,128)(2,1)S(1)}, bf16[16,1920]{1,0:T(8,128)(2,1)S(1)}, u32[]{:S(2)}, u32[]{:S(2)}) %collective-permute-start.2) | collective-permute-done | bytes 61472 | tf_op jit(solution)/shard_map/ppermute | solution.py:53
  10.4 2.8 %collective-permute-done.1.refs_2_ = bf16[16,1920]{1,0:T(8,128)(2,1)S(1)} collective-permute-done((bf16[16,1920]{1,0:T(8,128)(2,1)S(1)}, bf16[16,1920]{1,0:T(8,128)(2,1)S(1)}, u32[]{:S(2)}, u32[]{:S(2)}) %collective-permute-start.1) | collective-permute-done | bytes 61472 | tf_op jit(solution)/shard_map/ppermute | solution.py:53
  13.3 0.0 collective-permute-done.refs_1_
  13.3 0.8 copy-done
  14.1 2.6 %collective-permute-start.5 = (bf16[64,1920]{1,0:T(8,128)(2,1)S(1)}, bf16[64,1920]{1,0:T(8,128)(2,1)S(1)}, u32[]{:S(2)}, u32[]{:S(2)}) collective-permute-start(bf16[64,1920]{1,0:T(8,128)(2,1)S(1)} %get-tuple-element.43.refs_1_.refs_0_), channel_id=1, source_target_pairs={{0,6},{1,7},{2,4},{3,5},{4,2},{5,3},{6,0},{7,1},{8,14},{9,15},{10,... | collective-permute-start | bytes 737288 | tf_op jit(solution)/shard_map/ppermute | solution.py:53
  16.7 0.5 collective-permute-start.4
  17.2 0.4 collective-permute-start.3
  17.7 1.1 collective-permute-start.6
  18.8 3.1 %collective-permute-done.6.refs_1_ = bf16[16,1792]{1,0:T(8,128)(2,1)S(1)} collective-permute-done((bf16[16,1792]{1,0:T(8,128)(2,1)S(1)}, bf16[16,1792]{1,0:T(8,128)(2,1)S(1)}, u32[]{:S(2)}, u32[]{:S(2)}) %collective-permute-start.6) | collective-permute-done | bytes 57376 | tf_op jit(solution)/shard_map/ppermute | solution.py:53
  21.8 2.1 %collective-permute-done.5.refs_0_ = bf16[64,1920]{1,0:T(8,128)(2,1)S(1)} collective-permute-done((bf16[64,1920]{1,0:T(8,128)(2,1)S(1)}, bf16[64,1920]{1,0:T(8,128)(2,1)S(1)}, u32[]{:S(2)}, u32[]{:S(2)}) %collective-permute-start.5) | collective-permute-done | bytes 245792 | tf_op jit(solution)/shard_map/ppermute | solution.py:53
  24.0 0.1 collective-permute-start.10
  24.1 3.7 %collective-permute-done.4.refs_3_.refs_2_ = bf16[64,1920]{1,0:T(8,128)(2,1)S(1)} collective-permute-done((bf16[64,1920]{1,0:T(8,128)(2,1)S(1)}, bf16[64,1920]{1,0:T(8,128)(2,1)S(1)}, u32[]{:S(2)}, u32[]{:S(2)}) %collective-permute-start.4) | collective-permute-done | bytes 245792 | tf_op jit(solution)/shard_map/ppermute | solution.py:53
  27.8 0.0 collective-permute-start.9
  27.8 0.1 collective-permute-done.3.refs_2_.refs_1_
  27.9 0.4 collective-permute-start.8
  28.3 0.7 collective-permute-start.11
  29.0 7.5 %collective-permute-done.11.refs_1_ = bf16[32,1792]{1,0:T(8,128)(2,1)S(1)} collective-permute-done((bf16[32,1792]{1,0:T(8,128)(2,1)S(1)}, bf16[32,1792]{1,0:T(8,128)(2,1)S(1)}, u32[]{:S(2)}, u32[]{:S(2)}) %collective-permute-start.11) | collective-permute-done | bytes 114720 | tf_op jit(solution)/shard_map/ppermute | solution.py:53
  36.5 0.0 collective-permute-done.7.refs_5_.refs_4_
  36.5 0.0 collective-permute-done.10.refs_8_.refs_7_
  36.5 0.0 collective-permute-done.8.refs_6_.refs_5_
  36.6 0.1 collective-permute-start.16
  36.7 1.7 %collective-permute-start.15 = (bf16[64,1792]{1,0:T(8,128)(2,1)S(1)}, bf16[64,1792]{1,0:T(8,128)(2,1)S(1)}, u32[]{:S(2)}, u32[]{:S(2)}) collective-permute-start(bf16[64,1792]{1,0:T(8,128)(2,1)S(1)} %stack_cotangents.1.refs_10_.refs_0_), channel_id=1, source_target_pairs={{0,6},{1,7},{2,4},{3,5},{4,2},{5,3},{6,0},{7,1},{8,14},{9,15},{10,... | collective-permute-start | bytes 688136 | tf_op jit(solution)/shard_map/ppermute | solution.py:53
  38.4 1.3 %collective-permute-start.14 = (bf16[64,1792]{1,0:T(8,128)(2,1)S(1)}, bf16[64,1792]{1,0:T(8,128)(2,1)S(1)}, u32[]{:S(2)}, u32[]{:S(2)}) collective-permute-start(bf16[64,1792]{1,0:T(8,128)(2,1)S(1)} %stack_cotangents.1.refs_10_.refs_0_), channel_id=1, source_target_pairs={{0,2},{1,3},{2,0},{3,1},{4,6},{5,7},{6,4},{7,5},{8,10},{9,11},{10,... | collective-permute-start | bytes 688136 | tf_op jit(solution)/shard_map/ppermute | solution.py:53
  39.7 0.5 collective-permute-start.13
  40.2 16.6 %gate_up.1 = (bf16[4,64,1792]{2,1,0:T(8,128)(2,1)S(1)}, bf16[64,128]{1,0:T(8,128)(2,1)S(1)}, bf16[128,64]{1,0:T(8,128)(2,1)S(1)}, f32[64,128]{1,0:T(8,128)S(1)},...) custom-call(bf16[64,1920]{1,0:T(8,128)(2,1)S(1)} %get-tuple-element., ...), custom_call_target="tpu_custom_call" | custom-call | flops 46000001024 | tf_op jit(solution)/shard_map/gate_up/pallas_call | solution.py:83
  56.8 0.1 collective-permute-start.19
  56.9 0.0 collective-permute-done.14.refs_2_
  56.9 0.5 collective-permute-start.18
  57.4 0.1 collective-permute-start.17
  57.5 7.7 %forward.1 = (bf16[2,2,64,1792]{3,2,1,0:T(8,128)(2,1)S(1)}, bf16[2,2,64,1792]{3,2,1,0:T(8,128)(2,1)S(1)}) custom-call(bf16[64,1216]{1,0:T(8,128)(2,1)S(1)} %get-tuple-element.45.act_ref.refs_0_, f32[64,128]{1,0:T(8,128)S(1)} %get-tuple-element.46.gate_ref.refs_9_, bf16[128,64]{1,0:T(8,128)(2,1)S(1)} %get-tuple-element.47.back_ref, bf16[2,608,7168]{2,1,0:T(8,128)(2,1)} %refs_12_.1), custom_call_target="tpu_custom_call" | custom-call | flops 46000001024 | tf_op jit(solution)/shard_map/forward/pallas_call | solution.py:83
  65.2 0.5 collective-permute-start.12
  65.7 9.0 %hidden_grads.1 = (bf16[4,64,1792]{2,1,0:T(8,128)(2,1)S(1)}, bf16[64,1216]{1,0:T(8,128)(2,1)S(1)}, bf16[64,1216]{1,0:T(8,128)(2,1)S(1)}) custom-call(bf16[64,1792]{1,0:T(8,128)(2,1)S(1)} %stack_cotangents.1.refs_10_.refs_0_, bf16[64,1792]{1,0:T(8,128)(2,1)S(1)} %collective-permute-done.13.refs_1_, bf16[64,1792]{1,0:T(8,128)(2,1)S(1)} %collective-permute-done.14.refs_2_, ...), custom_call_target="tpu_custom_call" | custom-call | flops 46000001024 | tf_op jit(solution)/shard_map/hidden_grads/pallas_call | solution.py:83
  74.7 0.2 mixed_cores.1
  75.0 1.5 %collective-permute-start.20 = (bf16[64,1792]{1,0:T(8,128)(2,1)S(1)}, bf16[64,1792]{1,0:T(8,128)(2,1)S(1)}, u32[]{:S(2)}, u32[]{:S(2)}) collective-permute-start(bf16[64,1792]{1,0:T(8,128)(2,1)S(1)} %get-tuple-element.55), channel_id=1, source_target_pairs={{0,2},{1,3},{2,0},{3,1},{4,6},{5,7},{6,4},{7,5},{8,10},{9,11},{10,... | collective-permute-start | bytes 688136 | tf_op jit(solution)/shard_map/ppermute | solution.py:53
  76.5 0.8 collective-permute-start.21
  77.2 1.3 collective-permute-start.22
  78.5 11.2 %backward.1 = (bf16[2,2,64,1792]{3,2,1,0:T(8,128)(2,1)S(1)}, bf16[2,2,64,1792]{3,2,1,0:T(8,128)(2,1)S(1)}) custom-call(bf16[64,1216]{1,0:T(8,128)(2,1)S(1)} %get-tuple-element.53.refs_2_.dg_ref.refs_0_, bf16[64,1216]{1,0:T(8,128)(2,1)S(1)} %get-tuple-element.58.du_ref.refs_1_, bf16[128,64]{1,0:T(8,128)(2,1)S(1)} %get-tuple-element.47.back_ref, ...), custom_call_target="tpu_custom_call" | custom-call | flops 46000001024 | tf_op jit(solution)/shard_map/backward/pallas_call | solution.py:83
  89.7 0.1 collective-permute-start.23
  89.8 8.5 %grad_down.1 = (bf16[2,608,7168]{2,1,0:T(8,128)(2,1)}, f32[8,128]{1,0:T(8,128)S(1)}) custom-call(bf16[64,1216]{1,0:T(8,128)(2,1)S(1)} %get-tuple-element.45.act_ref.refs_0_, bf16[4,64,1792]{2,1,0:T(8,128)(2,1)S(1)} %get-tuple-element.62.refs_1_, bf16[2,2,64,1792]{3,2,1,0:T(8,128)(2,1)S(1)} %get-tuple-element.60.refs_2_.refs_0_), custom_call_target="tpu_custom_call" | custom-call | flops 46000001024 | tf_op jit(solution)/shard_map/grad_down/pallas_call | solution.py:83
  98.3 0.2 tokens_cores.1
  98.5 0.1 mixed_plane.1
  98.7 0.1 collective-permute-start.24
  98.7 2.4 %collective-permute-start.25 = (bf16[16,1792]{1,0:T(8,128)(2,1)S(1)}, bf16[16,1792]{1,0:T(8,128)(2,1)S(1)}, u32[]{:S(2)}, u32[]{:S(2)}) collective-permute-start(bf16[16,1792]{1,0:T(8,128)(2,1)S(1)} %get-tuple-element.67), channel_id=1, source_target_pairs={{0,16},{1,17},{2,18},{3,19},{4,20},{5,21},{6,22},{7,23},{8,24},{9,... | collective-permute-start | bytes 172040 | tf_op jit(solution)/shard_map/ppermute | solution.py:53
  101.2 1.5 %collective-permute-start.27 = (bf16[64,1792]{1,0:T(8,128)(2,1)S(1)}, bf16[64,1792]{1,0:T(8,128)(2,1)S(1)}, u32[]{:S(2)}, u32[]{:S(2)}) collective-permute-start(bf16[64,1792]{1,0:T(8,128)(2,1)S(1)} %get-tuple-element.71), channel_id=1, source_target_pairs={{0,2},{1,3},{2,0},{3,1},{4,6},{5,7},{6,4},{7,5},{8,10},{9,11},{10,... | collective-permute-start | bytes 688136 | tf_op jit(solution)/shard_map/ppermute | solution.py:53
  102.6 0.8 collective-permute-start.28
  103.4 1.2 collective-permute-start.29
  104.7 13.4 %grad_gate_up.1 = (bf16[2,608,7168]{2,1,0:T(8,128)(2,1)}, bf16[2,608,7168]{2,1,0:T(8,128)(2,1)}, f32[8,128]{1,0:T(8,128)S(1)}) custom-call(bf16[64,1216]{1,0:T(8,128)(2,1)S(1)} %get-tuple-element.53.refs_2_.dg_ref.refs_0_, bf16[64,1216]{1,0:T(8,128)(2,1)S(1)} %get-tuple-element.58.du_ref.refs_1_, bf16[4,64,1792]{2,1,0:T(8,128)(2,1)S(1)} %get-tuple-element.69.refs_2_, ...), custom_call_target="tpu_custom_call" | custom-call | flops 46000001024 | tf_op jit(solution)/shard_map/grad_gate_up/pallas_call | solution.py:83
  118.1 1.9 %collective-permute-start.26 = (bf16[16,1792]{1,0:T(8,128)(2,1)S(1)}, bf16[16,1792]{1,0:T(8,128)(2,1)S(1)}, u32[]{:S(2)}, u32[]{:S(2)}) collective-permute-start(bf16[16,1792]{1,0:T(8,128)(2,1)S(1)} %get-tuple-element.68), channel_id=1, source_target_pairs={{0,24},{1,25},{2,26},{3,27},{4,28},{5,29},{6,30},{7,31},{8,16},{9,... | collective-permute-start | bytes 172040 | tf_op jit(solution)/shard_map/ppermute | solution.py:53
  120.0 0.1 tokens_plane.1
  120.2 0.1 collective-permute-start.30
  120.2 2.4 %collective-permute-start.31 = (bf16[16,1792]{1,0:T(8,128)(2,1)S(1)}, bf16[16,1792]{1,0:T(8,128)(2,1)S(1)}, u32[]{:S(2)}, u32[]{:S(2)}) collective-permute-start(bf16[16,1792]{1,0:T(8,128)(2,1)S(1)} %get-tuple-element.76), channel_id=1, source_target_pairs={{0,16},{1,17},{2,18},{3,19},{4,20},{5,21},{6,22},{7,23},{8,24},{9,... | collective-permute-start | bytes 172040 | tf_op jit(solution)/shard_map/ppermute | solution.py:53
  122.7 1.9 %collective-permute-start.32 = (bf16[16,1792]{1,0:T(8,128)(2,1)S(1)}, bf16[16,1792]{1,0:T(8,128)(2,1)S(1)}, u32[]{:S(2)}, u32[]{:S(2)}) collective-permute-start(bf16[16,1792]{1,0:T(8,128)(2,1)S(1)} %get-tuple-element.77), channel_id=1, source_target_pairs={{0,24},{1,25},{2,26},{3,27},{4,28},{5,29},{6,30},{7,31},{8,16},{9,... | collective-permute-start | bytes 172040 | tf_op jit(solution)/shard_map/ppermute | solution.py:53
  124.6 0.2 collective-permute-done.26.refs_3_
  124.8 0.7 mixed_z.1
  125.4 0.7 collective-permute-done.31.refs_2_
  126.1 2.5 %collective-permute-done.32.refs_3_ = bf16[16,1792]{1,0:T(8,128)(2,1)S(1)} collective-permute-done((bf16[16,1792]{1,0:T(8,128)(2,1)S(1)}, bf16[16,1792]{1,0:T(8,128)(2,1)S(1)}, u32[]{:S(2)}, u32[]{:S(2)}) %collective-permute-start.32) | collective-permute-done | bytes 57376 | tf_op jit(solution)/shard_map/ppermute | solution.py:53
  128.7 0.7 tokens_z.1
  (28 shorter events, 0.1 us)
Async XLA Ops:
  0.6 0.8 copy-start.1
  1.5 0.7 copy-start.2
  2.1 0.7 copy-start.3
  2.9 7.5 %collective-permute-start.2 = (bf16[16,1920]{1,0:T(8,128)(2,1)S(1)}, bf16[16,1920]{1,0:T(8,128)(2,1)S(1)}, u32[]{:S(2)}, u32[]{:S(2)}) collective-permute-start(bf16[16,1920]{1,0:T(8,128)(2,1)S(1)} %pack.1.refs_0_), channel_id=1, source_target_pairs={{0,24},{1,25},{2,26},{3,27},{4,28},{5,29},{6,30},{7,31},{8,16},{9,... | collective-permute-start | bytes 184328 | tf_op jit(solution)/shard_map/ppermute | solution.py:53
  7.9 5.3 %collective-permute-start.1 = (bf16[16,1920]{1,0:T(8,128)(2,1)S(1)}, bf16[16,1920]{1,0:T(8,128)(2,1)S(1)}, u32[]{:S(2)}, u32[]{:S(2)}) collective-permute-start(bf16[16,1920]{1,0:T(8,128)(2,1)S(1)} %pack.1.refs_0_), channel_id=1, source_target_pairs={{0,16},{1,17},{2,18},{3,19},{4,20},{5,21},{6,22},{7,23},{8,24},{9,... | collective-permute-start | bytes 184328 | tf_op jit(solution)/shard_map/ppermute | solution.py:53
  7.9 5.3 %collective-permute-start = (bf16[16,1920]{1,0:T(8,128)(2,1)S(1)}, bf16[16,1920]{1,0:T(8,128)(2,1)S(1)}, u32[]{:S(2)}, u32[]{:S(2)}) collective-permute-start(bf16[16,1920]{1,0:T(8,128)(2,1)S(1)} %pack.1.refs_0_), channel_id=1, source_target_pairs={{0,8},{1,9},{2,10},{3,11},{4,12},{5,13},{6,14},{7,15},{8,0},{9,1},... | collective-permute-start | bytes 184328 | tf_op jit(solution)/shard_map/ppermute | solution.py:53
  13.3 0.8 copy-start
  14.1 9.9 %collective-permute-start.5 = (bf16[64,1920]{1,0:T(8,128)(2,1)S(1)}, bf16[64,1920]{1,0:T(8,128)(2,1)S(1)}, u32[]{:S(2)}, u32[]{:S(2)}) collective-permute-start(bf16[64,1920]{1,0:T(8,128)(2,1)S(1)} %get-tuple-element.43.refs_1_.refs_0_), channel_id=1, source_target_pairs={{0,6},{1,7},{2,4},{3,5},{4,2},{5,3},{6,0},{7,1},{8,14},{9,15},{10,... | collective-permute-start | bytes 737288 | tf_op jit(solution)/shard_map/ppermute | solution.py:53
  16.7 11.0 %collective-permute-start.4 = (bf16[64,1920]{1,0:T(8,128)(2,1)S(1)}, bf16[64,1920]{1,0:T(8,128)(2,1)S(1)}, u32[]{:S(2)}, u32[]{:S(2)}) collective-permute-start(bf16[64,1920]{1,0:T(8,128)(2,1)S(1)} %get-tuple-element.43.refs_1_.refs_0_), channel_id=1, source_target_pairs={{0,2},{1,3},{2,0},{3,1},{4,6},{5,7},{6,4},{7,5},{8,10},{9,11},{10,... | collective-permute-start | bytes 737288 | tf_op jit(solution)/shard_map/ppermute | solution.py:53
  17.2 10.6 %collective-permute-start.3 = (bf16[64,1920]{1,0:T(8,128)(2,1)S(1)}, bf16[64,1920]{1,0:T(8,128)(2,1)S(1)}, u32[]{:S(2)}, u32[]{:S(2)}) collective-permute-start(bf16[64,1920]{1,0:T(8,128)(2,1)S(1)} %get-tuple-element.43.refs_1_.refs_0_), channel_id=1, source_target_pairs={{0,4},{1,5},{2,6},{3,7},{4,0},{5,1},{6,2},{7,3},{8,12},{9,13},{10,... | collective-permute-start | bytes 737288 | tf_op jit(solution)/shard_map/ppermute | solution.py:53
  17.7 4.2 %collective-permute-start.6 = (bf16[16,1792]{1,0:T(8,128)(2,1)S(1)}, bf16[16,1792]{1,0:T(8,128)(2,1)S(1)}, u32[]{:S(2)}, u32[]{:S(2)}) collective-permute-start(bf16[16,1792]{1,0:T(8,128)(2,1)S(1)} %get-tuple-element.44.refs_0_), channel_id=1, source_target_pairs={{0,8},{1,9},{2,10},{3,11},{4,12},{5,13},{6,14},{7,15},{8,0},{9,1},... | collective-permute-start | bytes 172040 | tf_op jit(solution)/shard_map/ppermute | solution.py:53
  18.8 17.7 %collective-permute-start.7 = (bf16[64,1920]{1,0:T(8,128)(2,1)S(1)}, bf16[64,1920]{1,0:T(8,128)(2,1)S(1)}, u32[]{:S(2)}, u32[]{:S(2)}) collective-permute-start(bf16[64,1920]{1,0:T(8,128)(2,1)S(1)} %get-tuple-element.43.refs_1_.refs_0_), channel_id=1, source_target_pairs={{0,1},{1,0},{2,3},{3,2},{4,5},{5,4},{6,7},{7,6},{8,9},{9,8},{10,11... | collective-permute-start | bytes 737288 | tf_op jit(solution)/shard_map/ppermute | solution.py:53
  24.0 12.5 %collective-permute-start.10 = (bf16[64,1920]{1,0:T(8,128)(2,1)S(1)}, bf16[64,1920]{1,0:T(8,128)(2,1)S(1)}, u32[]{:S(2)}, u32[]{:S(2)}) collective-permute-start(bf16[64,1920]{1,0:T(8,128)(2,1)S(1)} %relay.1.refs_4_.refs_3_), channel_id=1, source_target_pairs={{0,1},{1,0},{2,3},{3,2},{4,5},{5,4},{6,7},{7,6},{8,9},{9,8},{10,11... | collective-permute-start | bytes 737288 | tf_op jit(solution)/shard_map/ppermute | solution.py:53
  27.8 8.8 %collective-permute-start.9 = (bf16[64,1920]{1,0:T(8,128)(2,1)S(1)}, bf16[64,1920]{1,0:T(8,128)(2,1)S(1)}, u32[]{:S(2)}, u32[]{:S(2)}) collective-permute-start(bf16[64,1920]{1,0:T(8,128)(2,1)S(1)} %collective-permute-done.4.refs_3_.refs_2_), channel_id=1, source_target_pairs={{0,1},{1,0},{2,3},{3,2},{4,5},{5,4},{6,7},{7,6},{8,9},{9,8},{10,11... | collective-permute-start | bytes 737288 | tf_op jit(solution)/shard_map/ppermute | solution.py:53
  27.9 8.7 %collective-permute-start.8 = (bf16[64,1920]{1,0:T(8,128)(2,1)S(1)}, bf16[64,1920]{1,0:T(8,128)(2,1)S(1)}, u32[]{:S(2)}, u32[]{:S(2)}) collective-permute-start(bf16[64,1920]{1,0:T(8,128)(2,1)S(1)} %collective-permute-done.3.refs_2_.refs_1_), channel_id=1, source_target_pairs={{0,1},{1,0},{2,3},{3,2},{4,5},{5,4},{6,7},{7,6},{8,9},{9,8},{10,11... | collective-permute-start | bytes 737288 | tf_op jit(solution)/shard_map/ppermute | solution.py:53
  28.3 8.2 %collective-permute-start.11 = (bf16[32,1792]{1,0:T(8,128)(2,1)S(1)}, bf16[32,1792]{1,0:T(8,128)(2,1)S(1)}, u32[]{:S(2)}, u32[]{:S(2)}) collective-permute-start(bf16[32,1792]{1,0:T(8,128)(2,1)S(1)} %double.2.refs_1_.refs_0_), channel_id=1, source_target_pairs={{0,16},{1,17},{2,18},{3,19},{4,20},{5,21},{6,22},{7,23},{8,24},{9,... | collective-permute-start | bytes 344072 | tf_op jit(solution)/shard_map/ppermute | solution.py:53
  36.6 29.1 %collective-permute-start.16 = (bf16[64,1792]{1,0:T(8,128)(2,1)S(1)}, bf16[64,1792]{1,0:T(8,128)(2,1)S(1)}, u32[]{:S(2)}, u32[]{:S(2)}) collective-permute-start(bf16[64,1792]{1,0:T(8,128)(2,1)S(1)} %stack_cotangents.1.refs_10_.refs_0_), channel_id=1, source_target_pairs={{0,1},{1,0},{2,3},{3,2},{4,5},{5,4},{6,7},{7,6},{8,9},{9,8},{10,11... | collective-permute-start | bytes 688136 | tf_op jit(solution)/shard_map/ppermute | solution.py:53
  36.7 20.2 %collective-permute-start.15 = (bf16[64,1792]{1,0:T(8,128)(2,1)S(1)}, bf16[64,1792]{1,0:T(8,128)(2,1)S(1)}, u32[]{:S(2)}, u32[]{:S(2)}) collective-permute-start(bf16[64,1792]{1,0:T(8,128)(2,1)S(1)} %stack_cotangents.1.refs_10_.refs_0_), channel_id=1, source_target_pairs={{0,6},{1,7},{2,4},{3,5},{4,2},{5,3},{6,0},{7,1},{8,14},{9,15},{10,... | collective-permute-start | bytes 688136 | tf_op jit(solution)/shard_map/ppermute | solution.py:53
  38.4 18.5 %collective-permute-start.14 = (bf16[64,1792]{1,0:T(8,128)(2,1)S(1)}, bf16[64,1792]{1,0:T(8,128)(2,1)S(1)}, u32[]{:S(2)}, u32[]{:S(2)}) collective-permute-start(bf16[64,1792]{1,0:T(8,128)(2,1)S(1)} %stack_cotangents.1.refs_10_.refs_0_), channel_id=1, source_target_pairs={{0,2},{1,3},{2,0},{3,1},{4,6},{5,7},{6,4},{7,5},{8,10},{9,11},{10,... | collective-permute-start | bytes 688136 | tf_op jit(solution)/shard_map/ppermute | solution.py:53
  39.7 17.7 %collective-permute-start.13 = (bf16[64,1792]{1,0:T(8,128)(2,1)S(1)}, bf16[64,1792]{1,0:T(8,128)(2,1)S(1)}, u32[]{:S(2)}, u32[]{:S(2)}) collective-permute-start(bf16[64,1792]{1,0:T(8,128)(2,1)S(1)} %stack_cotangents.1.refs_10_.refs_0_), channel_id=1, source_target_pairs={{0,4},{1,5},{2,6},{3,7},{4,0},{5,1},{6,2},{7,3},{8,12},{9,13},{10,... | collective-permute-start | bytes 688136 | tf_op jit(solution)/shard_map/ppermute | solution.py:53
  56.8 8.8 %collective-permute-start.19 = (bf16[64,1792]{1,0:T(8,128)(2,1)S(1)}, bf16[64,1792]{1,0:T(8,128)(2,1)S(1)}, u32[]{:S(2)}, u32[]{:S(2)}) collective-permute-start(bf16[64,1792]{1,0:T(8,128)(2,1)S(1)} %collective-permute-done.15.refs_3_), channel_id=1, source_target_pairs={{0,1},{1,0},{2,3},{3,2},{4,5},{5,4},{6,7},{7,6},{8,9},{9,8},{10,11... | collective-permute-start | bytes 688136 | tf_op jit(solution)/shard_map/ppermute | solution.py:53
  56.9 8.8 %collective-permute-start.18 = (bf16[64,1792]{1,0:T(8,128)(2,1)S(1)}, bf16[64,1792]{1,0:T(8,128)(2,1)S(1)}, u32[]{:S(2)}, u32[]{:S(2)}) collective-permute-start(bf16[64,1792]{1,0:T(8,128)(2,1)S(1)} %collective-permute-done.14.refs_2_), channel_id=1, source_target_pairs={{0,1},{1,0},{2,3},{3,2},{4,5},{5,4},{6,7},{7,6},{8,9},{9,8},{10,11... | collective-permute-start | bytes 688136 | tf_op jit(solution)/shard_map/ppermute | solution.py:53
  57.4 8.3 %collective-permute-start.17 = (bf16[64,1792]{1,0:T(8,128)(2,1)S(1)}, bf16[64,1792]{1,0:T(8,128)(2,1)S(1)}, u32[]{:S(2)}, u32[]{:S(2)}) collective-permute-start(bf16[64,1792]{1,0:T(8,128)(2,1)S(1)} %collective-permute-done.13.refs_1_), channel_id=1, source_target_pairs={{0,1},{1,0},{2,3},{3,2},{4,5},{5,4},{6,7},{7,6},{8,9},{9,8},{10,11... | collective-permute-start | bytes 688136 | tf_op jit(solution)/shard_map/ppermute | solution.py:53
  65.2 9.6 %collective-permute-start.12 = (bf16[2,2,64,1792]{3,2,1,0:T(8,128)(2,1)S(1)}, bf16[2,2,64,1792]{3,2,1,0:T(8,128)(2,1)S(1)}, u32[]{:S(2)}, u32[]{:S(2)}) collective-permute-start(bf16[2,2,64,1792]{3,2,1,0:T(8,128)(2,1)S(1)} %get-tuple-element.49), channel_id=1, source_target_pairs={{0,1},{1,0},{2,3},{3,2},{4,5},{5,4},{6,7},{7,6},{8,9},{9,8},{10,11... | collective-permute-start | bytes 2752520 | tf_op jit(solution)/shard_map/ppermute | solution.py:53
  75.0 23.6 %collective-permute-start.20 = (bf16[64,1792]{1,0:T(8,128)(2,1)S(1)}, bf16[64,1792]{1,0:T(8,128)(2,1)S(1)}, u32[]{:S(2)}, u32[]{:S(2)}) collective-permute-start(bf16[64,1792]{1,0:T(8,128)(2,1)S(1)} %get-tuple-element.55), channel_id=1, source_target_pairs={{0,2},{1,3},{2,0},{3,1},{4,6},{5,7},{6,4},{7,5},{8,10},{9,11},{10,... | collective-permute-start | bytes 688136 | tf_op jit(solution)/shard_map/ppermute | solution.py:53
  76.5 22.1 %collective-permute-start.21 = (bf16[64,1792]{1,0:T(8,128)(2,1)S(1)}, bf16[64,1792]{1,0:T(8,128)(2,1)S(1)}, u32[]{:S(2)}, u32[]{:S(2)}) collective-permute-start(bf16[64,1792]{1,0:T(8,128)(2,1)S(1)} %get-tuple-element.56), channel_id=1, source_target_pairs={{0,4},{1,5},{2,6},{3,7},{4,0},{5,1},{6,2},{7,3},{8,12},{9,13},{10,... | collective-permute-start | bytes 688136 | tf_op jit(solution)/shard_map/ppermute | solution.py:53
  77.2 21.3 %collective-permute-start.22 = (bf16[64,1792]{1,0:T(8,128)(2,1)S(1)}, bf16[64,1792]{1,0:T(8,128)(2,1)S(1)}, u32[]{:S(2)}, u32[]{:S(2)}) collective-permute-start(bf16[64,1792]{1,0:T(8,128)(2,1)S(1)} %get-tuple-element.57), channel_id=1, source_target_pairs={{0,6},{1,7},{2,4},{3,5},{4,2},{5,3},{6,0},{7,1},{8,14},{9,15},{10,... | collective-permute-start | bytes 688136 | tf_op jit(solution)/shard_map/ppermute | solution.py:53
  89.7 8.6 %collective-permute-start.23 = (bf16[2,2,64,1792]{3,2,1,0:T(8,128)(2,1)S(1)}, bf16[2,2,64,1792]{3,2,1,0:T(8,128)(2,1)S(1)}, u32[]{:S(2)}, u32[]{:S(2)}) collective-permute-start(bf16[2,2,64,1792]{3,2,1,0:T(8,128)(2,1)S(1)} %get-tuple-element.61), channel_id=1, source_target_pairs={{0,1},{1,0},{2,3},{3,2},{4,5},{5,4},{6,7},{7,6},{8,9},{9,8},{10,11... | collective-permute-start | bytes 2752520 | tf_op jit(solution)/shard_map/ppermute | solution.py:53
  98.7 24.0 %collective-permute-start.24 = (bf16[16,1792]{1,0:T(8,128)(2,1)S(1)}, bf16[16,1792]{1,0:T(8,128)(2,1)S(1)}, u32[]{:S(2)}, u32[]{:S(2)}) collective-permute-start(bf16[16,1792]{1,0:T(8,128)(2,1)S(1)} %get-tuple-element.66), channel_id=1, source_target_pairs={{0,8},{1,9},{2,10},{3,11},{4,12},{5,13},{6,14},{7,15},{8,0},{9,1},... | collective-permute-start | bytes 172040 | tf_op jit(solution)/shard_map/ppermute | solution.py:53
  98.7 25.9 %collective-permute-start.25 = (bf16[16,1792]{1,0:T(8,128)(2,1)S(1)}, bf16[16,1792]{1,0:T(8,128)(2,1)S(1)}, u32[]{:S(2)}, u32[]{:S(2)}) collective-permute-start(bf16[16,1792]{1,0:T(8,128)(2,1)S(1)} %get-tuple-element.67), channel_id=1, source_target_pairs={{0,16},{1,17},{2,18},{3,19},{4,20},{5,21},{6,22},{7,23},{8,24},{9,... | collective-permute-start | bytes 172040 | tf_op jit(solution)/shard_map/ppermute | solution.py:53
  101.2 16.9 %collective-permute-start.27 = (bf16[64,1792]{1,0:T(8,128)(2,1)S(1)}, bf16[64,1792]{1,0:T(8,128)(2,1)S(1)}, u32[]{:S(2)}, u32[]{:S(2)}) collective-permute-start(bf16[64,1792]{1,0:T(8,128)(2,1)S(1)} %get-tuple-element.71), channel_id=1, source_target_pairs={{0,2},{1,3},{2,0},{3,1},{4,6},{5,7},{6,4},{7,5},{8,10},{9,11},{10,... | collective-permute-start | bytes 688136 | tf_op jit(solution)/shard_map/ppermute | solution.py:53
  102.6 17.4 %collective-permute-start.28 = (bf16[64,1792]{1,0:T(8,128)(2,1)S(1)}, bf16[64,1792]{1,0:T(8,128)(2,1)S(1)}, u32[]{:S(2)}, u32[]{:S(2)}) collective-permute-start(bf16[64,1792]{1,0:T(8,128)(2,1)S(1)} %get-tuple-element.72), channel_id=1, source_target_pairs={{0,4},{1,5},{2,6},{3,7},{4,0},{5,1},{6,2},{7,3},{8,12},{9,13},{10,... | collective-permute-start | bytes 688136 | tf_op jit(solution)/shard_map/ppermute | solution.py:53
  103.4 16.6 %collective-permute-start.29 = (bf16[64,1792]{1,0:T(8,128)(2,1)S(1)}, bf16[64,1792]{1,0:T(8,128)(2,1)S(1)}, u32[]{:S(2)}, u32[]{:S(2)}) collective-permute-start(bf16[64,1792]{1,0:T(8,128)(2,1)S(1)} %get-tuple-element.73), channel_id=1, source_target_pairs={{0,6},{1,7},{2,4},{3,5},{4,2},{5,3},{6,0},{7,1},{8,14},{9,15},{10,... | collective-permute-start | bytes 688136 | tf_op jit(solution)/shard_map/ppermute | solution.py:53
  118.1 6.7 %collective-permute-start.26 = (bf16[16,1792]{1,0:T(8,128)(2,1)S(1)}, bf16[16,1792]{1,0:T(8,128)(2,1)S(1)}, u32[]{:S(2)}, u32[]{:S(2)}) collective-permute-start(bf16[16,1792]{1,0:T(8,128)(2,1)S(1)} %get-tuple-element.68), channel_id=1, source_target_pairs={{0,24},{1,25},{2,26},{3,27},{4,28},{5,29},{6,30},{7,31},{8,16},{9,... | collective-permute-start | bytes 172040 | tf_op jit(solution)/shard_map/ppermute | solution.py:53
  120.2 5.3 %collective-permute-start.30 = (bf16[16,1792]{1,0:T(8,128)(2,1)S(1)}, bf16[16,1792]{1,0:T(8,128)(2,1)S(1)}, u32[]{:S(2)}, u32[]{:S(2)}) collective-permute-start(bf16[16,1792]{1,0:T(8,128)(2,1)S(1)} %get-tuple-element.75), channel_id=1, source_target_pairs={{0,8},{1,9},{2,10},{3,11},{4,12},{5,13},{6,14},{7,15},{8,0},{9,1},... | collective-permute-start | bytes 172040 | tf_op jit(solution)/shard_map/ppermute | solution.py:53
  120.2 5.9 %collective-permute-start.31 = (bf16[16,1792]{1,0:T(8,128)(2,1)S(1)}, bf16[16,1792]{1,0:T(8,128)(2,1)S(1)}, u32[]{:S(2)}, u32[]{:S(2)}) collective-permute-start(bf16[16,1792]{1,0:T(8,128)(2,1)S(1)} %get-tuple-element.76), channel_id=1, source_target_pairs={{0,16},{1,17},{2,18},{3,19},{4,20},{5,21},{6,22},{7,23},{8,24},{9,... | collective-permute-start | bytes 172040 | tf_op jit(solution)/shard_map/ppermute | solution.py:53
  122.7 6.0 %collective-permute-start.32 = (bf16[16,1792]{1,0:T(8,128)(2,1)S(1)}, bf16[16,1792]{1,0:T(8,128)(2,1)S(1)}, u32[]{:S(2)}, u32[]{:S(2)}) collective-permute-start(bf16[16,1792]{1,0:T(8,128)(2,1)S(1)} %get-tuple-element.77), channel_id=1, source_target_pairs={{0,24},{1,25},{2,26},{3,27},{4,28},{5,29},{6,30},{7,31},{8,16},{9,... | collective-permute-start | bytes 172040 | tf_op jit(solution)/shard_map/ppermute | solution.py:53
